TPU v7x, 32 devices: a whole 2x2x4 slice. The times are simulated.
32 devices in a mesh: samp: 16 (over z, y, core), blk: 2 (over x).
Axes of the slice: x: 2, y: 2, z: 4, core: 2. Of those that a mesh axis runs over, the one named last changes fastest.
Arguments:
- genotypes: int32 [65536, 2048], P('samp', 'blk'), may hold values from 0 to 2
- traits: bfloat16 [65536, 64], P('samp'), may hold values from -6 to 6
- penalty_index: int32 [5], replicated, may hold values from 0 to 9
Outputs:
- level_gram: float32 [64, 10, 10], P('blk')
- level_cross: float32 [64, 10], P('blk')
All inputs are finite; a program needn't handle non-finite values.
Results may differ from a plain program's by a relative error of at most 0.0004.
Values may be sent and summed in bfloat16 or wider, within the bound.
No kernel may reach another device: no remote copies, remote signals or barrier semaphores. Data moves between devices by JAX's collectives and lax.ppermute only.
A program may use at most 192 MiB of HBM per device.

v0:
```python
import functools

import jax
import jax.numpy as jnp
from jax import lax
from jax.experimental import pallas as pl
from jax.experimental.pallas import tpu as pltpu
from jax.sharding import PartitionSpec as P

BLK = 128
SUB = 8
GROUP = 8
HI = lax.Precision.HIGHEST
NT = (((1,), (1,)), ((), ()))
TN = (((0,), (0,)), ((), ()))


def dot_hi(a, b):
    return jnp.dot(a, b, precision=HI, preferred_element_type=jnp.float32)


def dot_nt(a, b):
    return lax.dot_general(a, b, NT, precision=HI, preferred_element_type=jnp.float32)


def panel_rows(nvars):
    starts = [0]
    for j in range(nvars // BLK):
        starts.append(starts[-1] + nvars - BLK * j)
    return starts[:-1], starts[-1]


def side_rows(ntraits):
    return ntraits + SUB


def down(row):
    return jnp.transpose(jnp.broadcast_to(row, (BLK, BLK)))


def inverse_of(x):
    near = pl.reciprocal(x, approx=True)
    return near * (2.0 - x * near)


def split(x):
    first = x.astype(jnp.bfloat16)
    rest = x - first.astype(jnp.float32)
    second = rest.astype(jnp.bfloat16)
    return first, second, (rest - second.astype(jnp.float32)).astype(jnp.bfloat16)


def as_left(x):
    a, b, c = split(x)
    return jnp.concatenate([a, a, b, a, b, c], axis=1)


def as_right(x, axis):
    a, b, c = split(x)
    return jnp.concatenate([a, b, a, c, b, a], axis=axis)


def spread(x, lane):
    return jnp.broadcast_to(x[:, lane:lane + 1], (SUB, BLK))


def drop(x, row):
    return jnp.broadcast_to(x[row:row + 1, :], (SUB, BLK))


def total_of(terms):
    while len(terms) > 1:
        terms = [sum(terms[i:i + 2][1:], terms[i]) for i in range(0, len(terms), 2)]
    return terms[0]


def invert_pivots(cols, rows_at):
    for j in range(0, SUB, 2):
        a, b = drop(cols[j], j), drop(cols[j + 1], j)
        c, d = drop(cols[j], j + 1), drop(cols[j + 1], j + 1)
        scale = inverse_of(a * d - b * c)
        both = rows_at[j] | rows_at[j + 1]
        even = jnp.where(rows_at[j], -1.0, jnp.where(rows_at[j + 1], 0.0, cols[j]))
        odd = jnp.where(rows_at[j + 1], -1.0, jnp.where(rows_at[j], 0.0, cols[j + 1]))
        moved = []
        for i, x in enumerate(cols):
            if i == j:
                moved.append((odd * c - even * d) * scale)
            elif i == j + 1:
                moved.append((even * b - odd * a) * scale)
            else:
                above, below = drop(x, j), drop(x, j + 1)
                change = even * (d * above - b * below) + odd * (a * below - c * above)
                moved.append(jnp.where(both, 0.0, x) - change * scale)
        cols = moved
    return cols


def invert_tile(tile):
    count = BLK // SUB
    strips = [tile[SUB * i:SUB * (i + 1), :] for i in range(count)]
    lane = lax.broadcasted_iota(jnp.int32, (SUB, BLK), 1)
    sub = lax.broadcasted_iota(jnp.int32, (SUB, BLK), 0)
    rows_at = [sub == j for j in range(SUB)]
    cols = [spread(strips[0], j) for j in range(SUB)]
    for k in range(count):
        at = SUB * k
        inside = (lane >= at) & (lane < at + SUB)
        eye = (lane - at == sub).astype(jnp.float32)
        pivots = invert_pivots(cols, rows_at)
        own = jnp.where(inside, eye, strips[k])
        right = total_of([pivots[j] * drop(own, j) for j in range(SUB)])
        if k < count - 1:
            beside = [spread(strips[k + 1], at + j) for j in range(SUB)]
            mult = [total_of([beside[j] * drop(pivots[i], j) for j in range(SUB)]) for i in range(SUB)]
            after = []
            for j in range(SUB):
                above = spread(strips[k], at + SUB + j)
                below = spread(strips[k + 1], at + SUB + j)
                after.append(below - total_of([mult[i] * drop(above, i) for i in range(SUB)]))
            cols = after
        tops = [drop(right, j) for j in range(SUB)]
        fresh = []
        for i in range(count):
            if i == k:
                fresh.append(right)
                continue
            rest = jnp.where(inside, 0.0, strips[i])
            for j in range(SUB):
                rest = rest - spread(strips[i], at + j) * tops[j]
            fresh.append(rest)
        strips = fresh
    return jnp.concatenate(strips, axis=0)


def gram_kernel(ntraits, rank_ref, geno_ref, traits_ref, near_ref, away_ref, sent_ref, kept_ref, side, *panels):
    nvars = geno_ref.shape[1]
    step = pl.program_id(0)
    half = pl.num_programs(0) // 2
    wide = 2 * BLK

    @pl.when(step == 0)
    def _():
        side[...] = jnp.zeros_like(side)
        for panel in panels:
            panel[...] = jnp.zeros_like(panel)

    dosage = geno_ref[...].astype(jnp.float32).astype(jnp.bfloat16)

    @pl.when(step < half)
    def _():
        sent_ref[...] = dosage

    @pl.when(step >= half)
    def _():
        kept_ref[...] = dosage

    for j, panel in enumerate(panels):
        left, right = dosage[:, wide * j:], dosage[:, wide * j:wide * (j + 1)]
        panel[...] += lax.dot_general(left, right, TN, preferred_element_type=jnp.float32)
    traits = traits_ref[...]
    side[0:ntraits, :] += lax.dot_general(traits, dosage, TN, preferred_element_type=jnp.float32)
    ones = jnp.ones((SUB, dosage.shape[0]), jnp.bfloat16)
    sums = jnp.dot(ones, dosage, preferred_element_type=jnp.float32)
    ysum = jnp.dot(ones, traits, preferred_element_type=jnp.float32)
    ysum = jnp.concatenate([ysum, jnp.zeros((SUB, BLK - ntraits), jnp.float32)], axis=1)
    ysum = jnp.concatenate([ysum, jnp.zeros((SUB, nvars - BLK), jnp.float32)], axis=1)
    row = lax.broadcasted_iota(jnp.int32, (SUB, nvars), 0)
    side[ntraits:ntraits + SUB, :] += jnp.where(row == 0, sums, jnp.where(row == 1, ysum, 0.0))

    def hand_out(even, odd):
        rows = even.shape[0]

        def store(row, value):
            while value.shape[0] > 0:
                place, at = divmod(row, rows)
                size = min(value.shape[0], rows - at)
                (odd if place else even)[at:at + size, :] = value[:size, :]
                row, value = row + size, value[size:, :]

        starts, low = panel_rows(nvars)
        for j, start in enumerate(starts):
            skip = BLK * (j % 2)
            store(start, panels[j // 2][skip:, skip:skip + BLK])
        tall = side_rows(ntraits)
        for j in range(nvars // BLK):
            store(low + tall * j, side[:, BLK * j:BLK * (j + 1)])
        used = low + tall * (nvars // BLK)
        if used < 2 * rows:
            store(used, jnp.zeros((2 * rows - used, BLK), jnp.float32))

    last = step == pl.num_programs(0) - 1

    @pl.when(last & (rank_ref[1] == 0))
    def _():
        hand_out(near_ref, away_ref)

    @pl.when(last & (rank_ref[1] == 1))
    def _():
        hand_out(away_ref, near_ref)


def gram(genotypes, traits, place, members):
    count, nvars = genotypes.shape
    ntraits = traits.shape[1]
    steps = 4
    tile = count // steps
    half = steps // 2
    low = panel_rows(nvars)[1]
    share = 2 * SUB * members
    total = -(-(low + side_rows(ntraits) * (nvars // BLK)) // share) * share

    def source(i, place_ref):
        return (lax.rem(i + half * (1 - place_ref[0]), steps), 0)

    halves = jax.ShapeDtypeStruct((count // 2, nvars), jnp.bfloat16)
    return pl.pallas_call(
        functools.partial(gram_kernel, ntraits),
        grid_spec=pltpu.PrefetchScalarGridSpec(
            num_scalar_prefetch=1,
            grid=(steps,),
            in_specs=[pl.BlockSpec((tile, nvars), source), pl.BlockSpec((tile, ntraits), source)],
            out_specs=[
                pl.BlockSpec((total // 2, BLK), lambda i, rank_ref: (0, 0)),
                pl.BlockSpec((total // 2, BLK), lambda i, rank_ref: (0, 0)),
                pl.BlockSpec((tile, nvars), lambda i, rank_ref: (jnp.minimum(i, half - 1), 0)),
                pl.BlockSpec((tile, nvars), lambda i, rank_ref: (jnp.maximum(i - half, 0), 0)),
            ],
            scratch_shapes=[pltpu.VMEM((side_rows(ntraits), nvars), jnp.float32)]
            + [pltpu.VMEM((nvars - 2 * BLK * j, 2 * BLK), jnp.float32) for j in range(nvars // (2 * BLK))],
        ),
        out_shape=[jax.ShapeDtypeStruct((total // 2, BLK), jnp.float32)] * 2 + [halves, halves],
        compiler_params=pltpu.CompilerParams(vmem_limit_bytes=48 * 1024 * 1024),
        name="gram_sums",
    )(place, genotypes, traits)


def solve_kernel(nsamp, ntraits, lam_ref, near_a, near_b, far_a, far_b, coef_ref, mean_ref, aug, wide):
    nvars = coef_ref.shape[1]
    nblocks = nvars // BLK
    starts, low = panel_rows(nvars)
    tall = side_rows(ntraits)
    lam = lam_ref[0, 0]
    lower = lax.rem(lax.axis_index("samp"), 2) == 0
    quarter = near_a.shape[0]
    pairs = [(near_a, far_a), (near_b, far_b), (far_a, near_a), (far_b, near_b)]

    def read(row, count):
        found = []
        while count > 0:
            place, at = divmod(row, quarter)
            size = min(count, quarter - at)
            even, odd = pairs[place]
            found.append(jnp.where(lower, even[at:at + size, :], odd[at:at + size, :]))
            row, count = row + size, count - size
        return found[0] if len(found) == 1 else jnp.concatenate(found, axis=0)

    eye = lax.broadcasted_iota(jnp.int32, (BLK, BLK), 0) == lax.broadcasted_iota(jnp.int32, (BLK, BLK), 1)
    sides = [read(low + tall * j, tall) for j in range(nblocks)]
    means = [side[ntraits:ntraits + 1, :] / nsamp for side in sides]
    means_down = [down(mean) for mean in means]
    ysum = down(sides[0][ntraits + 1:ntraits + 2, :])[0:ntraits, :]
    for j in range(nblocks):
        span = slice(BLK * j, BLK * (j + 1))
        mean_ref[:, span] = jnp.broadcast_to(means[j], (SUB, BLK))
        for i in range(j, nblocks):
            value = read(starts[j] + BLK * (i - j), BLK) - nsamp * means_down[i] * means[j]
            if i == j:
                value = value + jnp.where(eye, lam * (value / nsamp + 1e-05), 0.0)
            aug[BLK * i:BLK * (i + 1), span] = value
        aug[nvars:nvars + ntraits, span] = sides[j][0:ntraits, :] - ysum * means[j]
    end = nvars + ntraits
    inverse = invert_tile(aug[0:BLK, 0:BLK])
    for k in range(nblocks):
        span = slice(BLK * k, BLK * (k + 1))
        first = BLK * (k + 1)
        panel = aug[first:end, span]
        mult = jnp.dot(as_left(panel), as_right(inverse, 0), preferred_element_type=jnp.float32)
        wide[first:end, span] = mult
        if k == nblocks - 1:
            break
        left, right = as_left(mult), as_right(panel, 1)
        j = k + 1
        while j < nblocks:
            top = BLK * j
            size = BLK if j == k + 1 or j == nblocks - 1 else 2 * BLK
            at = top - first
            aug[top:end, top:top + size] -= lax.dot_general(left[at:, :], right[at:at + size, :], NT, preferred_element_type=jnp.float32)
            if j == k + 1:
                inverse = invert_tile(aug[top:top + BLK, top:top + BLK])
            j += size // BLK
    solved = wide[nvars:end, nvars - BLK:nvars]
    coef_ref[:, nvars - BLK:nvars] = solved.astype(jnp.bfloat16)
    for k in range(nblocks - 2, -1, -1):
        span = slice(BLK * k, BLK * (k + 1))
        found = wide[nvars:end, span] - dot_hi(solved, wide[BLK * (k + 1):nvars, span])
        coef_ref[:, span] = found.astype(jnp.bfloat16)
        solved = jnp.concatenate([found, solved], axis=1)


def solve(pieces, lam, nsamp, nvars, ntraits):
    return pl.pallas_call(
        functools.partial(solve_kernel, nsamp, ntraits),
        out_shape=[jax.ShapeDtypeStruct((ntraits, nvars), jnp.bfloat16), jax.ShapeDtypeStruct((SUB, nvars), jnp.float32)],
        in_specs=[pl.BlockSpec(memory_space=pltpu.SMEM)] + [pl.BlockSpec(memory_space=pltpu.VMEM)] * 4,
        out_specs=[pl.BlockSpec(memory_space=pltpu.VMEM)] * 2,
        scratch_shapes=[
            pltpu.VMEM((nvars + ntraits, nvars), jnp.float32),
            pltpu.VMEM((nvars + ntraits, nvars), jnp.float32),
        ],
        compiler_params=pltpu.CompilerParams(vmem_limit_bytes=48 * 1024 * 1024),
        cost_estimate=pl.CostEstimate(flops=10**6, bytes_accessed=10**6, transcendentals=0),
        name="ridge_solve",
    )(lam, *pieces)


def level_kernel(npen, own_ref, other_ref, coef_ref, mean_ref, far_mean_ref, traits_ref, out_ref, pred):
    rank = lax.axis_index("blk")
    ntraits = coef_ref.shape[2]
    nvars = own_ref.shape[1]
    count = own_ref.shape[0]
    stack = 2 * npen
    tile = 512
    for place in range(2):
        block = rank if place == 0 else 1 - rank
        source = own_ref if place == 0 else other_ref
        mean = (mean_ref if place == 0 else far_mean_ref)[0:1, :]
        coef = jnp.concatenate([coef_ref[r, block] for r in range(npen)], axis=0)
        offset = jnp.sum(coef.astype(jnp.float32) * mean, axis=1, keepdims=True)
        low = pl.multiple_of(block * (npen * ntraits), npen * ntraits)
        for n in range(0, count, tile):
            value = lax.dot_general(coef, source[n:n + tile, :], NT, preferred_element_type=jnp.float32)
            pred[pl.ds(low, npen * ntraits), n:n + tile] = value - offset
    for n in range(0, count, tile):
        rows = traits_ref[n:n + tile, :].astype(jnp.float32)
        rows = jnp.concatenate([rows, jnp.zeros((tile, BLK - ntraits), jnp.float32)], axis=1)
        pred[stack * ntraits:(stack + 1) * ntraits, n:n + tile] = jnp.transpose(rows)[0:ntraits, :]
    lane = lax.broadcasted_iota(jnp.int32, (SUB, BLK), 1)
    for t in range(0, ntraits, SUB):
        acc = jnp.zeros((SUB, BLK), jnp.float32)
        for i in range(stack):
            left = pred[i * ntraits + t:i * ntraits + t + SUB, :]
            for j in range(i, stack + 1):
                term = jnp.sum(left * pred[j * ntraits + t:j * ntraits + t + SUB, :], axis=1, keepdims=True)
                if j < stack:
                    acc = jnp.where((lane == i * stack + j) | (lane == j * stack + i), term, acc)
                else:
                    acc = jnp.where(lane == stack * stack + i, term, acc)
        out_ref[t:t + SUB, :] = acc


def level_sums(own, other, coefs, mean, far_mean, traits, npen):
    ntraits = traits.shape[1]
    count = own.shape[0]
    return pl.pallas_call(
        functools.partial(level_kernel, npen),
        out_shape=jax.ShapeDtypeStruct((ntraits, BLK), jnp.float32),
        in_specs=[pl.BlockSpec(memory_space=pltpu.VMEM)] * 6,
        out_specs=pl.BlockSpec(memory_space=pltpu.VMEM),
        scratch_shapes=[pltpu.VMEM(((2 * npen + 1) * ntraits, count), jnp.float32)],
        compiler_params=pltpu.CompilerParams(vmem_limit_bytes=56 * 1024 * 1024),
        name="level_sums",
    )(own, other, coefs, mean, far_mean, traits)


def swapped(x, bit):
    return lax.ppermute(x, "samp", [(i, i ^ (1 << bit)) for i in range(lax.axis_size("samp"))])


def place_bit(bit):
    return lax.rem(lax.div(lax.axis_index("samp"), 1 << bit), 2)


def halved(x, bit):
    rows = x.shape[0] // 2
    mine = place_bit(bit)
    far = swapped(lax.dynamic_slice_in_dim(x, (1 - mine) * rows, rows, 0), bit)
    return lax.dynamic_slice_in_dim(x, mine * rows, rows, 0) + far


def doubled(x, bit):
    far = swapped(x, bit)
    even = place_bit(bit) == 0
    return jnp.concatenate([jnp.where(even, x, far), jnp.where(even, far, x)], axis=0)


def all_sums(x, away):
    bits = list(range(1, lax.axis_size("samp").bit_length() - 1))
    x = x + swapped(away, 0)
    rows = x.shape[0] // 2
    near = []
    for part, order in ((x[:rows], bits), (x[rows:], bits[1:] + bits[:1])):
        for bit in order:
            part = halved(part, bit)
        for bit in reversed(order):
            part = doubled(part, bit)
        near.append(part)
    return near + [swapped(part, 0) for part in near]


def small_sum(x):
    for bit in range(lax.axis_size("samp").bit_length() - 1):
        x = x + swapped(x, bit)
    return x


def level_from_predictions(coefs, mean, dosage, traits, nvars):
    coef = coefs.transpose(0, 2, 1)
    ntraits = traits.shape[1]
    offset = jnp.einsum("rmt,m->rt", coef.astype(jnp.float32), mean, precision=HI)
    pred = jnp.einsum("rmt,nm->trn", coef, dosage, preferred_element_type=jnp.float32)
    pred = (pred - offset.T[:, :, None]).astype(jnp.bfloat16)
    local_traits = ntraits // lax.axis_size("blk")
    parts = lax.all_to_all(pred[None], "blk", split_axis=1, concat_axis=0, tiled=True)
    mine = lax.dynamic_slice_in_dim(traits, lax.axis_index("blk") * local_traits, local_traits, 1)
    gram = jnp.einsum("btrn,ctsn->tbrcs", parts, parts, preferred_element_type=jnp.float32)
    cross = jnp.einsum("btrn,nt->tbr", parts, mine, preferred_element_type=jnp.float32)
    count, stack = parts.shape[1], parts.shape[0] * parts.shape[2]
    gram, cross = lax.psum((gram.reshape(count, stack, stack), cross.reshape(count, stack)), "samp")
    return gram / nvars, cross / nvars


def local(genotypes, traits, penalty_index):
    count, nvars = genotypes.shape
    ntraits = traits.shape[1]
    npen = penalty_index.shape[0]
    nblk = lax.axis_size("blk")
    members = lax.axis_size("samp")
    nsamp = float(count * members)
    samp_rank = lax.axis_index("samp")
    blk_rank = lax.axis_index("blk")
    paired = nblk == 2
    place = jnp.stack([blk_rank if paired else jnp.int32(0), place_bit(0)])
    near, away, sent, kept = gram(genotypes, traits, place, members)
    if paired:
        other = lax.ppermute(sent, "blk", [(0, 1), (1, 0)])
    pieces = all_sums(near, away)
    lam = nsamp * jnp.exp2((penalty_index.astype(jnp.float32) - 8.0) / 2.0)
    mine = lax.dynamic_index_in_dim(lam, (samp_rank % GROUP) % npen, 0, keepdims=True).reshape(1, 1)
    coef, mean = solve(pieces, mine, nsamp, nvars, ntraits)
    groups = [list(range(g, g + GROUP)) for g in range(0, members, GROUP)]
    if not paired:
        coefs = lax.all_gather(coef, "samp", axis_index_groups=groups)[:npen]
        dosage = genotypes.astype(jnp.bfloat16)
        return level_from_predictions(coefs, mean[0], dosage, traits, nvars)
    coef_far = lax.ppermute(coef, "blk", [(0, 1), (1, 0)])
    mean_far = lax.ppermute(mean, "blk", [(0, 1), (1, 0)])
    first = blk_rank == 0
    both = jnp.stack([jnp.where(first, coef, coef_far), jnp.where(first, coef_far, coef)])
    coefs = lax.all_gather(both, "samp", axis_index_groups=groups)
    rows = lax.dynamic_slice_in_dim(traits, blk_rank * (count // 2), count // 2, 0)
    found = level_sums(kept, other, coefs, mean, mean_far, rows, npen)
    stack = nblk * npen
    each = ntraits // nblk
    far = lax.ppermute(lax.dynamic_slice_in_dim(found, (1 - blk_rank) * each, each, 0), "blk", [(0, 1), (1, 0)])
    found = small_sum(lax.dynamic_slice_in_dim(found, blk_rank * each, each, 0) + far) / nvars
    return found[:, :stack * stack].reshape(each, stack, stack), found[:, stack * stack:stack * stack + stack]


def solution(mesh):
    placed = (P("samp", "blk"), P("samp", None), P())
    return jax.shard_map(
        local,
        mesh=mesh,
        in_specs=placed,
        out_specs=(P("blk", None, None), P("blk", None)),
        check_vma=False,
    )
```

profile of v0, /device:TPU:0, one launch (start us, length us, event | category | flops | bytes accessed | tf_op | source)
XLA Modules:
  0.0 241.7 jit_solution(11507059077464984057)
XLA Ops:
  7.2 1.5 copy.13.traits_ref
  8.8 17.4 %gram_sums.1 = (f32[2688,128]{1,0:T(8,128)S(1)}, f32[2688,128]{1,0:T(8,128)}, bf16[2048,1024]{1,0:T(8,128)(2,1)}, bf16[2048,1024]{1,0:T(8,128)(2,1)}) custom-call(s32[2]{0:T(128)S(1)} %pad_add_fusion.rank_ref, s32[4096,1024]{1,0:T(8,128)} %geno_ref.1, bf16[4096,64]{1,0:T(8,128)(2,1)S(1)} %copy.13.traits_ref), custom_call_target="tpu_custom_call" | custom-call | tf_op jit(solution)/shard_map/gram_sums/pallas_call | solution.py:217
  26.2 0.6 collective-permute-start.1
  26.8 3.1 %collective-permute-done.1 = f32[2688,128]{1,0:T(8,128)} collective-permute-done((f32[2688,128]{1,0:T(8,128)}, f32[2688,128]{1,0:T(8,128)}, u32[]{:S(2)}, u32[]{:S(2)}) %collective-permute-start.1) | collective-permute-done | bytes 1376288 | tf_op jit(solution)/shard_map/ppermute | solution.py:367
  29.9 1.5 add.96
  31.6 2.9 %collective-permute-start.8 = (f32[672,128]{1,0:T(8,128)S(1)}, f32[672,128]{1,0:T(8,128)S(1)}, u32[]{:S(2)}, u32[]{:S(2)}) collective-permute-start(f32[672,128]{1,0:T(8,128)S(1)} %constant_dynamic-slice_fusion.4), channel_id=1, source_target_pairs={{0,8},{2,10},{4,12},{6,14},{8,0},{10,2},{12,4},{14,6},{16,24},{18,... | collective-permute-start | bytes 1032200 | tf_op jit(solution)/shard_map/ppermute | solution.py:367
  34.5 1.6 collective-permute-start.2
  36.1 6.8 %collective-permute-done.8 = f32[672,128]{1,0:T(8,128)S(1)} collective-permute-done((f32[672,128]{1,0:T(8,128)S(1)}, f32[672,128]{1,0:T(8,128)S(1)}, u32[]{:S(2)}, u32[]{:S(2)}) %collective-permute-start.8) | collective-permute-done | bytes 344096 | tf_op jit(solution)/shard_map/ppermute | solution.py:367
  42.9 2.8 %collective-permute-start.9 = (f32[336,128]{1,0:T(8,128)S(1)}, f32[336,128]{1,0:T(8,128)S(1)}, u32[]{:S(2)}, u32[]{:S(2)}) collective-permute-start(f32[336,128]{1,0:T(8,128)S(1)} %constant_dynamic-slice_fusion.3), channel_id=1, source_target_pairs={{0,16},{2,18},{4,20},{6,22},{8,24},{10,26},{12,28},{14,30},{16,0},... | collective-permute-start | bytes 516104 | tf_op jit(solution)/shard_map/ppermute | solution.py:367
  45.8 1.6 collective-permute-start.3
  47.4 6.1 %collective-permute-done.9 = f32[336,128]{1,0:T(8,128)S(1)} collective-permute-done((f32[336,128]{1,0:T(8,128)S(1)}, f32[336,128]{1,0:T(8,128)S(1)}, u32[]{:S(2)}, u32[]{:S(2)}) %collective-permute-start.9) | collective-permute-done | bytes 172064 | tf_op jit(solution)/shard_map/ppermute | solution.py:367
  53.6 1.4 collective-permute-start.10
  55.1 0.6 collective-permute-start.4
  55.7 2.4 %collective-permute-done.10 = f32[168,128]{1,0:T(8,128)S(1)} collective-permute-done((f32[168,128]{1,0:T(8,128)S(1)}, f32[168,128]{1,0:T(8,128)S(1)}, u32[]{:S(2)}, u32[]{:S(2)}) %collective-permute-start.10) | collective-permute-done | bytes 86048 | tf_op jit(solution)/shard_map/ppermute | solution.py:367
  58.2 1.4 collective-permute-start.11
  59.6 2.9 %collective-permute-done.4 = f32[168,128]{1,0:T(8,128)S(1)} collective-permute-done((f32[168,128]{1,0:T(8,128)S(1)}, f32[168,128]{1,0:T(8,128)S(1)}, u32[]{:S(2)}, u32[]{:S(2)}) %collective-permute-start.4) | collective-permute-done | bytes 86048 | tf_op jit(solution)/shard_map/ppermute | solution.py:367
  62.6 0.1 collective-permute-done.11
  62.8 2.9 %collective-permute-start.12 = (f32[336,128]{1,0:T(8,128)S(1)}, f32[336,128]{1,0:T(8,128)S(1)}, u32[]{:S(2)}, u32[]{:S(2)}) collective-permute-start(f32[336,128]{1,0:T(8,128)S(1)} %pad_maximum_fusion.6), channel_id=1, source_target_pairs={{0,16},{2,18},{4,20},{6,22},{8,24},{10,26},{12,28},{14,30},{16,0},... | collective-permute-start | bytes 516104 | tf_op jit(solution)/shard_map/ppermute | solution.py:367
  65.6 6.3 %collective-permute-done.5 = f32[168,128]{1,0:T(8,128)S(1)} collective-permute-done((f32[168,128]{1,0:T(8,128)S(1)}, f32[168,128]{1,0:T(8,128)S(1)}, u32[]{:S(2)}, u32[]{:S(2)}) %collective-permute-start.5) | collective-permute-done | bytes 86048 | tf_op jit(solution)/shard_map/ppermute | solution.py:367
  72.0 1.7 collective-permute-done.12
  73.8 0.4 collective-permute-start.13
  74.2 5.2 %collective-permute-done.6 = f32[336,128]{1,0:T(8,128)S(1)} collective-permute-done((f32[336,128]{1,0:T(8,128)S(1)}, f32[336,128]{1,0:T(8,128)S(1)}, u32[]{:S(2)}, u32[]{:S(2)}) %collective-permute-start.6) | collective-permute-done | bytes 172064 | tf_op jit(solution)/shard_map/ppermute | solution.py:367
  79.5 3.8 %collective-permute-done.13 = f32[672,128]{1,0:T(8,128)S(1)} collective-permute-done((f32[672,128]{1,0:T(8,128)S(1)}, f32[672,128]{1,0:T(8,128)S(1)}, u32[]{:S(2)}, u32[]{:S(2)}) %collective-permute-start.13) | collective-permute-done | bytes 344096 | tf_op jit(solution)/shard_map/ppermute | solution.py:367
  83.5 3.2 %collective-permute-done.7 = f32[672,128]{1,0:T(8,128)S(1)} collective-permute-done((f32[672,128]{1,0:T(8,128)S(1)}, f32[672,128]{1,0:T(8,128)S(1)}, u32[]{:S(2)}, u32[]{:S(2)}) %collective-permute-start.7) | collective-permute-done | bytes 344096 | tf_op jit(solution)/shard_map/ppermute | solution.py:367
  86.9 1.6 collective-permute-start
  88.5 0.6 dynamic_slice.49
  89.2 54.5 %ridge_solve.1 = (bf16[64,1024]{1,0:T(8,128)(2,1)S(1)}, f32[8,1024]{1,0:T(8,128)S(1)}) custom-call(f32[1,1]{1,0:T(1,128)} %bitcast.2.lam_ref, f32[1344,128]{1,0:T(8,128)S(1)} %pad_maximum_fusion.near_a, f32[1344,128]{1,0:T(8,128)S(1)} %pad_maximum_fusion.1.near_b, f32[1344,128]{1,0:T(8,128)} %collective-permute-done.14.far_a, ...), custom_call_target="tpu_custom_call" | custom-call | flops 1000000 | bytes 1000000 | tf_op jit(solution)/shard_map/ridge_solve/pallas_call | solution.py:302
  143.7 1.6 collective-permute-start.16
  145.2 37.7 %collective-permute-done.16 = bf16[64,1024]{1,0:T(8,128)(2,1)S(1)} collective-permute-done((bf16[64,1024]{1,0:T(8,128)(2,1)S(1)}, bf16[64,1024]{1,0:T(8,128)(2,1)S(1)}, u32[]{:S(2)}, u32[]{:S(2)}) %collective-permute-start.16) | collective-permute-done | bytes 131104 | tf_op jit(solution)/shard_map/ppermute | solution.py:446
  182.9 0.7 pad_maximum_fusion.4
  183.7 1.6 collective-permute-start.17
  185.2 0.8 constant_dynamic-slice_fusion.1.traits_ref
  186.1 1.6 collective-permute-done.17.far_mean_ref
  187.7 16.8 %all-gather.3.cloned.1.call-done = bf16[16,64,1024]{2,1,0:T(8,128)(2,1)} async-done(((bf16[2,64,1024]{2,1,0:T(8,128)(2,1)}), bf16[16,64,1024]{2,1,0:T(8,128)(2,1)}) %all-gather.3.cloned.1.call-update) | async-done | bytes 2097168 | tf_op jit(solution)/shard_map/all_gather | solution.py:450
  204.5 10.1 %level_sums.1 = f32[64,128]{1,0:T(8,128)} custom-call(bf16[2048,1024]{1,0:T(8,128)(2,1)} %get-tuple-element.8.own_ref, bf16[2048,1024]{1,0:T(8,128)(2,1)} %collective-permute-done.other_ref, bf16[8,2,64,1024]{3,2,1,0:T(8,128)(2,1)} %bitcast.11, f32[8,1024]{1,0:T(8,128)} %copy-done, f32[8,1024]{1,0:T(8,128)} %copy-done.1, ...), custom_call_target="tpu_custom_call" | custom-call | tf_op jit(solution)/shard_map/level_sums/pallas_call | solution.py:355
  214.6 0.7 constant_dynamic-slice_fusion
  215.4 1.6 collective-permute-start.18
  217.0 2.1 collective-permute-done.18
  219.1 0.7 dynamic-slice_add_fusion.6
  219.8 1.2 collective-permute-done.19
  221.0 1.5 collective-permute-start.20
  222.5 2.2 collective-permute-done.20
  224.7 1.6 collective-permute-start.21
  226.3 2.1 collective-permute-done.21
  228.5 2.6 %collective-permute-start.22 = (f32[32,128]{1,0:T(8,128)S(1)}, f32[32,128]{1,0:T(8,128)S(1)}, u32[]{:S(2)}, u32[]{:S(2)}) collective-permute-start(f32[32,128]{1,0:T(8,128)S(1)} %add.121), channel_id=1, source_target_pairs={{0,16},{2,18},{4,20},{6,22},{8,24},{10,26},{12,28},{14,30},{16,0},... | collective-permute-start | bytes 49160 | tf_op jit(solution)/shard_map/ppermute | solution.py:367
  231.1 2.1 collective-permute-done.22
  233.2 0.7 copy.16
  234.0 0.6 reshape.11
  (53 shorter events, 1.5 us)
Async XLA Ops:
  7.2 197.3 %all-gather.3.cloned.1.call-start = ((), (), s32[]{:S(2)}) async-start(), calls=%async_computation | async-start | bytes 2359296 | tf_op jit(solution)/shard_map/all_gather | solution.py:450
  26.2 3.7 %collective-permute-start.1 = (f32[2688,128]{1,0:T(8,128)}, f32[2688,128]{1,0:T(8,128)}, u32[]{:S(2)}, u32[]{:S(2)}) collective-permute-start(f32[2688,128]{1,0:T(8,128)} %get-tuple-element.11), channel_id=1, source_target_pairs={{0,2},{2,0},{4,6},{6,4},{8,10},{10,8},{12,14},{14,12},{16,18},{18,... | collective-permute-start | bytes 4128776 | tf_op jit(solution)/shard_map/ppermute | solution.py:367
  31.6 11.3 %collective-permute-start.8 = (f32[672,128]{1,0:T(8,128)S(1)}, f32[672,128]{1,0:T(8,128)S(1)}, u32[]{:S(2)}, u32[]{:S(2)}) collective-permute-start(f32[672,128]{1,0:T(8,128)S(1)} %constant_dynamic-slice_fusion.4), channel_id=1, source_target_pairs={{0,8},{2,10},{4,12},{6,14},{8,0},{10,2},{12,4},{14,6},{16,24},{18,... | collective-permute-start | bytes 1032200 | tf_op jit(solution)/shard_map/ppermute | solution.py:367
  34.5 11.2 %collective-permute-start.2 = (f32[672,128]{1,0:T(8,128)S(1)}, f32[672,128]{1,0:T(8,128)S(1)}, u32[]{:S(2)}, u32[]{:S(2)}) collective-permute-start(f32[672,128]{1,0:T(8,128)S(1)} %constant_dynamic-slice_fusion.7), channel_id=1, source_target_pairs={{0,4},{2,6},{4,0},{6,2},{8,12},{10,14},{12,8},{14,10},{16,20},{18,... | collective-permute-start | bytes 1032200 | tf_op jit(solution)/shard_map/ppermute | solution.py:367
  42.9 10.7 %collective-permute-start.9 = (f32[336,128]{1,0:T(8,128)S(1)}, f32[336,128]{1,0:T(8,128)S(1)}, u32[]{:S(2)}, u32[]{:S(2)}) collective-permute-start(f32[336,128]{1,0:T(8,128)S(1)} %constant_dynamic-slice_fusion.3), channel_id=1, source_target_pairs={{0,16},{2,18},{4,20},{6,22},{8,24},{10,26},{12,28},{14,30},{16,0},... | collective-permute-start | bytes 516104 | tf_op jit(solution)/shard_map/ppermute | solution.py:367
  45.8 9.2 %collective-permute-start.3 = (f32[336,128]{1,0:T(8,128)S(1)}, f32[336,128]{1,0:T(8,128)S(1)}, u32[]{:S(2)}, u32[]{:S(2)}) collective-permute-start(f32[336,128]{1,0:T(8,128)S(1)} %constant_dynamic-slice_fusion.6), channel_id=1, source_target_pairs={{0,8},{2,10},{4,12},{6,14},{8,0},{10,2},{12,4},{14,6},{16,24},{18,... | collective-permute-start | bytes 516104 | tf_op jit(solution)/shard_map/ppermute | solution.py:367
  53.6 4.6 %collective-permute-start.10 = (f32[168,128]{1,0:T(8,128)S(1)}, f32[168,128]{1,0:T(8,128)S(1)}, u32[]{:S(2)}, u32[]{:S(2)}) collective-permute-start(f32[168,128]{1,0:T(8,128)S(1)} %constant_dynamic-slice_fusion.2), channel_id=1, source_target_pairs={{0,4},{2,6},{4,0},{6,2},{8,12},{10,14},{12,8},{14,10},{16,20},{18,... | collective-permute-start | bytes 258056 | tf_op jit(solution)/shard_map/ppermute | solution.py:367
  55.1 7.4 %collective-permute-start.4 = (f32[168,128]{1,0:T(8,128)S(1)}, f32[168,128]{1,0:T(8,128)S(1)}, u32[]{:S(2)}, u32[]{:S(2)}) collective-permute-start(f32[168,128]{1,0:T(8,128)S(1)} %constant_dynamic-slice_fusion.5), channel_id=1, source_target_pairs={{0,16},{2,18},{4,20},{6,22},{8,24},{10,26},{12,28},{14,30},{16,0},... | collective-permute-start | bytes 258056 | tf_op jit(solution)/shard_map/ppermute | solution.py:367
  58.2 4.6 %collective-permute-start.11 = (f32[168,128]{1,0:T(8,128)S(1)}, f32[168,128]{1,0:T(8,128)S(1)}, u32[]{:S(2)}, u32[]{:S(2)}) collective-permute-start(f32[168,128]{1,0:T(8,128)S(1)} %dynamic-slice_add_fusion.4), channel_id=1, source_target_pairs={{0,4},{2,6},{4,0},{6,2},{8,12},{10,14},{12,8},{14,10},{16,20},{18,... | collective-permute-start | bytes 258056 | tf_op jit(solution)/shard_map/ppermute | solution.py:367
  62.5 9.4 %collective-permute-start.5 = (f32[168,128]{1,0:T(8,128)S(1)}, f32[168,128]{1,0:T(8,128)S(1)}, u32[]{:S(2)}, u32[]{:S(2)}) collective-permute-start(f32[168,128]{1,0:T(8,128)S(1)} %dynamic-slice_add_fusion.5), channel_id=1, source_target_pairs={{0,16},{2,18},{4,20},{6,22},{8,24},{10,26},{12,28},{14,30},{16,0},... | collective-permute-start | bytes 258056 | tf_op jit(solution)/shard_map/ppermute | solution.py:367
  62.8 11.0 %collective-permute-start.12 = (f32[336,128]{1,0:T(8,128)S(1)}, f32[336,128]{1,0:T(8,128)S(1)}, u32[]{:S(2)}, u32[]{:S(2)}) collective-permute-start(f32[336,128]{1,0:T(8,128)S(1)} %pad_maximum_fusion.6), channel_id=1, source_target_pairs={{0,16},{2,18},{4,20},{6,22},{8,24},{10,26},{12,28},{14,30},{16,0},... | collective-permute-start | bytes 516104 | tf_op jit(solution)/shard_map/ppermute | solution.py:367
  72.0 7.4 %collective-permute-start.6 = (f32[336,128]{1,0:T(8,128)S(1)}, f32[336,128]{1,0:T(8,128)S(1)}, u32[]{:S(2)}, u32[]{:S(2)}) collective-permute-start(f32[336,128]{1,0:T(8,128)S(1)} %pad_maximum_fusion.5), channel_id=1, source_target_pairs={{0,8},{2,10},{4,12},{6,14},{8,0},{10,2},{12,4},{14,6},{16,24},{18,... | collective-permute-start | bytes 516104 | tf_op jit(solution)/shard_map/ppermute | solution.py:367
  73.8 9.5 %collective-permute-start.13 = (f32[672,128]{1,0:T(8,128)S(1)}, f32[672,128]{1,0:T(8,128)S(1)}, u32[]{:S(2)}, u32[]{:S(2)}) collective-permute-start(f32[672,128]{1,0:T(8,128)S(1)} %pad_maximum_fusion.3), channel_id=1, source_target_pairs={{0,8},{2,10},{4,12},{6,14},{8,0},{10,2},{12,4},{14,6},{16,24},{18,... | collective-permute-start | bytes 1032200 | tf_op jit(solution)/shard_map/ppermute | solution.py:367
  79.4 7.3 %collective-permute-start.7 = (f32[672,128]{1,0:T(8,128)S(1)}, f32[672,128]{1,0:T(8,128)S(1)}, u32[]{:S(2)}, u32[]{:S(2)}) collective-permute-start(f32[672,128]{1,0:T(8,128)S(1)} %pad_maximum_fusion.2), channel_id=1, source_target_pairs={{0,4},{2,6},{4,0},{6,2},{8,12},{10,14},{12,8},{14,10},{16,20},{18,... | collective-permute-start | bytes 1032200 | tf_op jit(solution)/shard_map/ppermute | solution.py:367
  83.4 5.1 %copy-start.2 = (s32[5]{0:T(128)S(1)}, s32[5]{0:T(128)}, u32[]{:S(2)}) copy-start(s32[5]{0:T(128)} %param.5) | copy-start | bytes 64
  83.4 5.7 %collective-permute-start.15 = (f32[1344,128]{1,0:T(8,128)S(1)}, f32[1344,128]{1,0:T(8,128)S(1)}, u32[]{:S(2)}, u32[]{:S(2)}) collective-permute-start(f32[1344,128]{1,0:T(8,128)S(1)} %pad_maximum_fusion.1.near_b), channel_id=1, source_target_pairs={{0,2},{2,0},{4,6},{6,4},{8,10},{10,8},{12,14},{14,12},{16,18},{18,... | collective-permute-start | bytes 2064392 | tf_op jit(solution)/shard_map/ppermute | solution.py:367
  86.8 2.3 collective-permute-start.14
  86.9 100.8 %collective-permute-start = (bf16[2048,1024]{1,0:T(8,128)(2,1)}, bf16[2048,1024]{1,0:T(8,128)(2,1)}, u32[]{:S(2)}, u32[]{:S(2)}) collective-permute-start(bf16[2048,1024]{1,0:T(8,128)(2,1)} %get-tuple-element.9), channel_id=1, source_target_pairs={{0,1},{1,0},{2,3},{3,2},{4,5},{5,4},{6,7},{7,6},{8,9},{9,8},{10,11... | collective-permute-start | bytes 12582920 | tf_op jit(solution)/shard_map/ppermute | solution.py:436
  143.7 60.8 %copy-start = (f32[8,1024]{1,0:T(8,128)}, f32[8,1024]{1,0:T(8,128)S(1)}, u32[]{:S(2)}) copy-start(f32[8,1024]{1,0:T(8,128)S(1)} %get-tuple-element.13.mean_ref) | copy-start | bytes 98308
  143.7 39.2 %collective-permute-start.16 = (bf16[64,1024]{1,0:T(8,128)(2,1)S(1)}, bf16[64,1024]{1,0:T(8,128)(2,1)S(1)}, u32[]{:S(2)}, u32[]{:S(2)}) collective-permute-start(bf16[64,1024]{1,0:T(8,128)(2,1)S(1)} %get-tuple-element.12), channel_id=1, source_target_pairs={{0,1},{1,0},{2,3},{3,2},{4,5},{5,4},{6,7},{7,6},{8,9},{9,8},{10,11... | collective-permute-start | bytes 393224 | tf_op jit(solution)/shard_map/ppermute | solution.py:446
  183.7 4.0 %collective-permute-start.17 = (f32[8,1024]{1,0:T(8,128)S(1)}, f32[8,1024]{1,0:T(8,128)S(1)}, u32[]{:S(2)}, u32[]{:S(2)}) collective-permute-start(f32[8,1024]{1,0:T(8,128)S(1)} %get-tuple-element.13.mean_ref), channel_id=1, source_target_pairs={{0,1},{1,0},{2,3},{3,2},{4,5},{5,4},{6,7},{7,6},{8,9},{9,8},{10,11... | collective-permute-start | bytes 98312 | tf_op jit(solution)/shard_map/ppermute | solution.py:447
  187.7 16.8 %copy-start.1 = (f32[8,1024]{1,0:T(8,128)}, f32[8,1024]{1,0:T(8,128)S(1)}, u32[]{:S(2)}) copy-start(f32[8,1024]{1,0:T(8,128)S(1)} %collective-permute-done.17.far_mean_ref) | copy-start | bytes 98308
  215.4 3.7 %collective-permute-start.18 = (f32[32,128]{1,0:T(8,128)S(1)}, f32[32,128]{1,0:T(8,128)S(1)}, u32[]{:S(2)}, u32[]{:S(2)}) collective-permute-start(f32[32,128]{1,0:T(8,128)S(1)} %constant_dynamic-slice_fusion), channel_id=1, source_target_pairs={{0,1},{1,0},{2,3},{3,2},{4,5},{5,4},{6,7},{7,6},{8,9},{9,8},{10,11... | collective-permute-start | bytes 49160 | tf_op jit(solution)/shard_map/ppermute | solution.py:455
  219.8 1.2 collective-permute-start.19
  221.0 3.7 %collective-permute-start.20 = (f32[32,128]{1,0:T(8,128)S(1)}, f32[32,128]{1,0:T(8,128)S(1)}, u32[]{:S(2)}, u32[]{:S(2)}) collective-permute-start(f32[32,128]{1,0:T(8,128)S(1)} %add.119), channel_id=1, source_target_pairs={{0,4},{2,6},{4,0},{6,2},{8,12},{10,14},{12,8},{14,10},{16,20},{18,... | collective-permute-start | bytes 49160 | tf_op jit(solution)/shard_map/ppermute | solution.py:367
  224.7 3.7 %collective-permute-start.21 = (f32[32,128]{1,0:T(8,128)S(1)}, f32[32,128]{1,0:T(8,128)S(1)}, u32[]{:S(2)}, u32[]{:S(2)}) collective-permute-start(f32[32,128]{1,0:T(8,128)S(1)} %add.120), channel_id=1, source_target_pairs={{0,8},{2,10},{4,12},{6,14},{8,0},{10,2},{12,4},{14,6},{16,24},{18,... | collective-permute-start | bytes 49160 | tf_op jit(solution)/shard_map/ppermute | solution.py:367
  228.5 4.6 %collective-permute-start.22 = (f32[32,128]{1,0:T(8,128)S(1)}, f32[32,128]{1,0:T(8,128)S(1)}, u32[]{:S(2)}, u32[]{:S(2)}) collective-permute-start(f32[32,128]{1,0:T(8,128)S(1)} %add.121), channel_id=1, source_target_pairs={{0,16},{2,18},{4,20},{6,22},{8,24},{10,26},{12,28},{14,30},{16,0},... | collective-permute-start | bytes 49160 | tf_op jit(solution)/shard_map/ppermute | solution.py:367
Sparse Core Ops, SparseCore 0:
  183.8 20.6 all-gather.2
where the time goes:
time: 245 us; the launch traced here: 242 us
  waiting for transfers between devices  108 us (44%)
  Pallas kernels  82 us (33%)
  starting transfers between devices  28.7 us (12%)
  between operations  14.5 us (6%)
  local copies, waits for them, and re-layouts  5.4 us (2%)
  other arithmetic  3.55 us (1%)
    pallas_call x1, Pallas kernels, solve(): pl.pallas_call(functools.partial(solve_kernel, nsamp, ntraits), out_shape...  54.5 us
    ppermute x19, waiting for transfers between devices, swapped(): lax.ppermute(x, 'samp', [(i, i ^ 1 << bit) for i in range(lax.axis_size('...  49.4 us
    ppermute x1, waiting for transfers between devices, local(): coef_far = lax.ppermute(coef, 'blk', [(0, 1), (1, 0)])  37.7 us
    ppermute x19, starting transfers between devices, swapped(): lax.ppermute(x, 'samp', [(i, i ^ 1 << bit) for i in range(lax.axis_size('...  22.3 us
    pallas_call x1, Pallas kernels, gram(): pl.pallas_call(functools.partial(gram_kernel, ntraits), grid_spec=pltpu.P...  17.4 us
    all_gather x1, waiting for transfers between devices, local(): coefs = lax.all_gather(both, 'samp', axis_index_groups=groups)  16.8 us
    pallas_call x1, Pallas kernels, level_sums(): pl.pallas_call(functools.partial(level_kernel, npen), out_shape=jax.Shape...  10.1 us
  transfers between devices with their start and end apart: 24, of which 20 were waited for; matrix products, arithmetic and copies ran while one was open for 1% of the time, Pallas kernels for 23%

commit v1 on v0

--- a/solution.py
+++ b/solution.py
@@ -74,7 +74,7 @@
     return terms[0]
 
 
-def invert_pivots(cols, rows_at):
+def solve_pivots(cols, right, rows_at):
     for j in range(0, SUB, 2):
         a, b = drop(cols[j], j), drop(cols[j + 1], j)
         c, d = drop(cols[j], j + 1), drop(cols[j + 1], j + 1)
@@ -82,18 +82,16 @@
         both = rows_at[j] | rows_at[j + 1]
         even = jnp.where(rows_at[j], -1.0, jnp.where(rows_at[j + 1], 0.0, cols[j]))
         odd = jnp.where(rows_at[j + 1], -1.0, jnp.where(rows_at[j], 0.0, cols[j + 1]))
-        moved = []
-        for i, x in enumerate(cols):
-            if i == j:
-                moved.append((odd * c - even * d) * scale)
-            elif i == j + 1:
-                moved.append((even * b - odd * a) * scale)
-            else:
-                above, below = drop(x, j), drop(x, j + 1)
-                change = even * (d * above - b * below) + odd * (a * below - c * above)
-                moved.append(jnp.where(both, 0.0, x) - change * scale)
-        cols = moved
-    return cols
+        above_by = even * d - odd * c
+        below_by = odd * a - even * b
+
+        def move(x):
+            change = above_by * drop(x, j) + below_by * drop(x, j + 1)
+            return jnp.where(both, 0.0, x) - change * scale
+
+        cols = cols[:j + 2] + [move(x) for x in cols[j + 2:]]
+        right = move(right)
+    return right
 
 
 def invert_tile(tile):
@@ -102,33 +100,20 @@
     lane = lax.broadcasted_iota(jnp.int32, (SUB, BLK), 1)
     sub = lax.broadcasted_iota(jnp.int32, (SUB, BLK), 0)
     rows_at = [sub == j for j in range(SUB)]
-    cols = [spread(strips[0], j) for j in range(SUB)]
     for k in range(count):
         at = SUB * k
         inside = (lane >= at) & (lane < at + SUB)
         eye = (lane - at == sub).astype(jnp.float32)
-        pivots = invert_pivots(cols, rows_at)
-        own = jnp.where(inside, eye, strips[k])
-        right = total_of([pivots[j] * drop(own, j) for j in range(SUB)])
-        if k < count - 1:
-            beside = [spread(strips[k + 1], at + j) for j in range(SUB)]
-            mult = [total_of([beside[j] * drop(pivots[i], j) for j in range(SUB)]) for i in range(SUB)]
-            after = []
-            for j in range(SUB):
-                above = spread(strips[k], at + SUB + j)
-                below = spread(strips[k + 1], at + SUB + j)
-                after.append(below - total_of([mult[i] * drop(above, i) for i in range(SUB)]))
-            cols = after
+        cols = [spread(strips[k], at + j) for j in range(SUB)]
+        right = solve_pivots(cols, jnp.where(inside, eye, strips[k]), rows_at)
         tops = [drop(right, j) for j in range(SUB)]
         fresh = []
         for i in range(count):
             if i == k:
                 fresh.append(right)
-                continue
-            rest = jnp.where(inside, 0.0, strips[i])
-            for j in range(SUB):
-                rest = rest - spread(strips[i], at + j) * tops[j]
-            fresh.append(rest)
+            else:
+                change = total_of([spread(strips[i], at + j) * tops[j] for j in range(SUB)])
+                fresh.append(jnp.where(inside, 0.0, strips[i]) - change)
         strips = fresh
     return jnp.concatenate(strips, axis=0)
 
@@ -314,15 +299,19 @@
     )(lam, *pieces)
 
 
-def level_kernel(npen, own_ref, other_ref, coef_ref, mean_ref, far_mean_ref, traits_ref, out_ref, pred):
+def level_kernel(npen, own_ref, halves_ref, coef_ref, mean_ref, far_mean_ref, traits_ref, out_ref, pred, other_ref, sem):
     rank = lax.axis_index("blk")
     ntraits = coef_ref.shape[2]
     nvars = own_ref.shape[1]
     count = own_ref.shape[0]
     stack = 2 * npen
     tile = 512
+    fetch = pltpu.make_async_copy(halves_ref.at[1 - rank], other_ref, sem)
+    fetch.start()
     for place in range(2):
         block = rank if place == 0 else 1 - rank
+        if place == 1:
+            fetch.wait()
         source = own_ref if place == 0 else other_ref
         mean = (mean_ref if place == 0 else far_mean_ref)[0:1, :]
         coef = jnp.concatenate([coef_ref[r, block] for r in range(npen)], axis=0)
@@ -349,18 +338,23 @@
         out_ref[t:t + SUB, :] = acc
 
 
-def level_sums(own, other, coefs, mean, far_mean, traits, npen):
+def level_sums(own, halves, coefs, mean, far_mean, traits, npen):
     ntraits = traits.shape[1]
     count = own.shape[0]
+    vmem = pl.BlockSpec(memory_space=pltpu.VMEM)
     return pl.pallas_call(
         functools.partial(level_kernel, npen),
         out_shape=jax.ShapeDtypeStruct((ntraits, BLK), jnp.float32),
-        in_specs=[pl.BlockSpec(memory_space=pltpu.VMEM)] * 6,
+        in_specs=[vmem, pl.BlockSpec(memory_space=pl.ANY)] + [vmem] * 4,
         out_specs=pl.BlockSpec(memory_space=pltpu.VMEM),
-        scratch_shapes=[pltpu.VMEM(((2 * npen + 1) * ntraits, count), jnp.float32)],
+        scratch_shapes=[
+            pltpu.VMEM(((2 * npen + 1) * ntraits, count), jnp.float32),
+            pltpu.VMEM(own.shape, own.dtype),
+            pltpu.SemaphoreType.DMA,
+        ],
         compiler_params=pltpu.CompilerParams(vmem_limit_bytes=56 * 1024 * 1024),
         name="level_sums",
-    )(own, other, coefs, mean, far_mean, traits)
+    )(own, halves, coefs, mean, far_mean, traits)
 
 
 def swapped(x, bit):
@@ -433,7 +427,7 @@
     place = jnp.stack([blk_rank if paired else jnp.int32(0), place_bit(0)])
     near, away, sent, kept = gram(genotypes, traits, place, members)
     if paired:
-        other = lax.ppermute(sent, "blk", [(0, 1), (1, 0)])
+        halves = lax.all_gather(sent, "blk")
     pieces = all_sums(near, away)
     lam = nsamp * jnp.exp2((penalty_index.astype(jnp.float32) - 8.0) / 2.0)
     mine = lax.dynamic_index_in_dim(lam, (samp_rank % GROUP) % npen, 0, keepdims=True).reshape(1, 1)
@@ -449,7 +443,7 @@
     both = jnp.stack([jnp.where(first, coef, coef_far), jnp.where(first, coef_far, coef)])
     coefs = lax.all_gather(both, "samp", axis_index_groups=groups)
     rows = lax.dynamic_slice_in_dim(traits, blk_rank * (count // 2), count // 2, 0)
-    found = level_sums(kept, other, coefs, mean, mean_far, rows, npen)
+    found = level_sums(kept, halves, coefs, mean, mean_far, rows, npen)
     stack = nblk * npen
     each = ntraits // nblk
     far = lax.ppermute(lax.dynamic_slice_in_dim(found, (1 - blk_rank) * each, each, 0), "blk", [(0, 1), (1, 0)])

time: 245 us -> 321 us (1.31)
  waiting for transfers between devices: 108 us -> 183 us
  Pallas kernels: 82 us -> 85.5 us
    all_gather x0 -> x1, waiting for transfers between devices: none -> 106 us  [local(): halves = lax.all_gather(sent, 'blk')]
    ppermute x1, waiting for transfers between devices: 37.7 us -> 4.05 us  [local(): coef_far = lax.ppermute(coef, 'blk', [(0, 1), (1, 0)])]
    pallas_call x1, Pallas kernels: 54.5 us -> 58.6 us  [solve(): pl.pallas_call(functools.partial(solve_kernel, nsamp, ntraits), out_shape...]
  transfers between devices with their start and end apart: 24 -> 24, of which waited for: 20 -> 21; matrix products, arithmetic and copies ran while one was open for 1% -> 1% of each run, Pallas kernels for 23% -> 0%
where the time goes in v1:
time: 321 us; the launch traced here: 317 us
  waiting for transfers between devices  183 us (57%)
  Pallas kernels  85.5 us (27%)
  starting transfers between devices  25.7 us (8%)
  between operations  14.5 us (5%)
  local copies, waits for them, and re-layouts  5.4 us (2%)
  other arithmetic  3.56 us (1%)
    all_gather x1, waiting for transfers between devices, local(): halves = lax.all_gather(sent, 'blk')  106 us
    pallas_call x1, Pallas kernels, solve(): pl.pallas_call(functools.partial(solve_kernel, nsamp, ntraits), out_shape...  58.6 us
    ppermute x19, waiting for transfers between devices, swapped(): lax.ppermute(x, 'samp', [(i, i ^ 1 << bit) for i in range(lax.axis_size('...  51.2 us
    ppermute x19, starting transfers between devices, swapped(): lax.ppermute(x, 'samp', [(i, i ^ 1 << bit) for i in range(lax.axis_size('...  22 us
    pallas_call x1, Pallas kernels, gram(): pl.pallas_call(functools.partial(gram_kernel, ntraits), grid_spec=pltpu.P...  17.4 us
    all_gather x1, waiting for transfers between devices, local(): coefs = lax.all_gather(both, 'samp', axis_index_groups=groups)  16 us
    pallas_call x1, Pallas kernels, level_sums(): pl.pallas_call(functools.partial(level_kernel, npen), out_shape=jax.Shape...  9.6 us
  transfers between devices with their start and end apart: 24, of which 21 were waited for; matrix products, arithmetic and copies ran while one was open for 1% of the time, Pallas kernels for 0%

profile of v1, /device:TPU:0, one launch (start us, length us, event | category | flops | bytes accessed | tf_op | source)
XLA Modules:
  0.0 317.3 jit_solution(7717159251817746697)
XLA Ops:
  7.2 1.5 copy.13.traits_ref
  8.8 17.4 %gram_sums.1 = (f32[2688,128]{1,0:T(8,128)S(1)}, f32[2688,128]{1,0:T(8,128)}, bf16[2048,1024]{1,0:T(8,128)(2,1)}, bf16[2048,1024]{1,0:T(8,128)(2,1)}) custom-call(s32[2]{0:T(128)S(1)} %pad_add_fusion.rank_ref, s32[4096,1024]{1,0:T(8,128)} %geno_ref.1, bf16[4096,64]{1,0:T(8,128)(2,1)S(1)} %copy.13.traits_ref), custom_call_target="tpu_custom_call" | custom-call | tf_op jit(solution)/shard_map/gram_sums/pallas_call | solution.py:202
  26.2 0.6 collective-permute-start
  26.8 3.1 collective-permute-done
  29.9 1.5 add.96
  31.5 2.9 collective-permute-start.7
  34.5 1.6 collective-permute-start.1
  36.0 6.8 %collective-permute-done.7 = f32[672,128]{1,0:T(8,128)S(1)} collective-permute-done((f32[672,128]{1,0:T(8,128)S(1)}, f32[672,128]{1,0:T(8,128)S(1)}, u32[]{:S(2)}, u32[]{:S(2)}) %collective-permute-start.7) | collective-permute-done | bytes 344096 | tf_op jit(solution)/shard_map/ppermute | solution.py:361
  42.9 2.8 collective-permute-start.8
  45.8 1.6 collective-permute-start.2
  47.4 6.1 %collective-permute-done.8 = f32[336,128]{1,0:T(8,128)S(1)} collective-permute-done((f32[336,128]{1,0:T(8,128)S(1)}, f32[336,128]{1,0:T(8,128)S(1)}, u32[]{:S(2)}, u32[]{:S(2)}) %collective-permute-start.8) | collective-permute-done | bytes 172064 | tf_op jit(solution)/shard_map/ppermute | solution.py:361
  53.6 1.4 collective-permute-start.9
  55.1 0.6 collective-permute-start.3
  55.7 2.4 collective-permute-done.9
  58.1 1.4 collective-permute-start.10
  59.6 2.9 collective-permute-done.3
  62.7 2.9 collective-permute-start.11
  65.6 6.3 %collective-permute-done.4 = f32[168,128]{1,0:T(8,128)S(1)} collective-permute-done((f32[168,128]{1,0:T(8,128)S(1)}, f32[168,128]{1,0:T(8,128)S(1)}, u32[]{:S(2)}, u32[]{:S(2)}) %collective-permute-start.4) | collective-permute-done | bytes 86048 | tf_op jit(solution)/shard_map/ppermute | solution.py:361
  72.0 1.7 collective-permute-done.11
  73.8 0.4 collective-permute-start.12
  74.1 5.2 %collective-permute-done.5 = f32[336,128]{1,0:T(8,128)S(1)} collective-permute-done((f32[336,128]{1,0:T(8,128)S(1)}, f32[336,128]{1,0:T(8,128)S(1)}, u32[]{:S(2)}, u32[]{:S(2)}) %collective-permute-start.5) | collective-permute-done | bytes 172064 | tf_op jit(solution)/shard_map/ppermute | solution.py:361
  79.4 3.8 %collective-permute-done.12 = f32[672,128]{1,0:T(8,128)S(1)} collective-permute-done((f32[672,128]{1,0:T(8,128)S(1)}, f32[672,128]{1,0:T(8,128)S(1)}, u32[]{:S(2)}, u32[]{:S(2)}) %collective-permute-start.12) | collective-permute-done | bytes 344096 | tf_op jit(solution)/shard_map/ppermute | solution.py:361
  83.5 3.2 %collective-permute-done.6 = f32[672,128]{1,0:T(8,128)S(1)} collective-permute-done((f32[672,128]{1,0:T(8,128)S(1)}, f32[672,128]{1,0:T(8,128)S(1)}, u32[]{:S(2)}, u32[]{:S(2)}) %collective-permute-start.6) | collective-permute-done | bytes 344096 | tf_op jit(solution)/shard_map/ppermute | solution.py:361
  86.9 0.6 dynamic_slice.49
  87.5 1.6 collective-permute-done.13.far_a
  89.1 58.6 %ridge_solve.1 = (bf16[64,1024]{1,0:T(8,128)(2,1)S(1)}, f32[8,1024]{1,0:T(8,128)S(1)}) custom-call(f32[1,1]{1,0:T(1,128)} %bitcast.3.lam_ref, f32[1344,128]{1,0:T(8,128)S(1)} %pad_maximum_fusion.near_a, f32[1344,128]{1,0:T(8,128)S(1)} %pad_maximum_fusion.1.near_b, f32[1344,128]{1,0:T(8,128)} %collective-permute-done.13.far_a, ...), custom_call_target="tpu_custom_call" | custom-call | flops 1000000 | bytes 1000000 | tf_op jit(solution)/shard_map/ridge_solve/pallas_call | solution.py:287
  147.7 1.6 collective-permute-start.15
  149.3 4.1 %collective-permute-done.15 = bf16[64,1024]{1,0:T(8,128)(2,1)S(1)} collective-permute-done((bf16[64,1024]{1,0:T(8,128)(2,1)S(1)}, bf16[64,1024]{1,0:T(8,128)(2,1)S(1)}, u32[]{:S(2)}, u32[]{:S(2)}) %collective-permute-start.15) | collective-permute-done | bytes 131104 | tf_op jit(solution)/shard_map/ppermute | solution.py:440
  153.4 0.7 pad_maximum_fusion.4
  154.3 0.5 all-gather.5.cloned.1.call-update
  154.9 1.6 collective-permute-start.16
  156.4 0.8 constant_dynamic-slice_fusion.1.traits_ref
  157.3 1.6 collective-permute-done.16.far_mean_ref
  158.9 16.0 %all-gather.7.cloned.1.call-done = bf16[16,64,1024]{2,1,0:T(8,128)(2,1)} async-done(((bf16[2,64,1024]{2,1,0:T(8,128)(2,1)}), bf16[16,64,1024]{2,1,0:T(8,128)(2,1)}) %all-gather.7.cloned.1.call-update) | async-done | bytes 2097168 | tf_op jit(solution)/shard_map/all_gather | solution.py:444
  174.9 105.7 %all-gather.5.cloned.1.call-done = bf16[4096,1024]{1,0:T(8,128)(2,1)} async-done(((bf16[2048,1024]{1,0:T(8,128)(2,1)}), bf16[4096,1024]{1,0:T(8,128)(2,1)}) %all-gather.5.cloned.1.call-update) | async-done | bytes 8388624 | tf_op jit(solution)/shard_map/all_gather | solution.py:430
  280.6 9.6 %level_sums.1 = f32[64,128]{1,0:T(8,128)} custom-call(bf16[2048,1024]{1,0:T(8,128)(2,1)} %get-tuple-element.8.own_ref, bf16[2,2048,1024]{2,1,0:T(8,128)(2,1)} %bitcast.12, bf16[8,2,64,1024]{3,2,1,0:T(8,128)(2,1)} %bitcast.13, f32[8,1024]{1,0:T(8,128)} %copy-done, f32[8,1024]{1,0:T(8,128)} %copy-done.1, bf16[2048,64]{1,0:T(8,128)(2,1)} %constant_dynamic-slice_fusion.1.traits_ref), custom_call_target="tpu_custom_call" | custom-call | tf_op jit(solution)/shard_map/level_sums/pallas_call | solution.py:345
  290.2 0.7 constant_dynamic-slice_fusion
  291.3 3.4 %collective-permute-done.17 = f32[32,128]{1,0:T(8,128)S(1)} collective-permute-done((f32[32,128]{1,0:T(8,128)S(1)}, f32[32,128]{1,0:T(8,128)S(1)}, u32[]{:S(2)}, u32[]{:S(2)}) %collective-permute-start.17) | collective-permute-done | bytes 16416 | tf_op jit(solution)/shard_map/ppermute | solution.py:449
  294.7 0.7 dynamic-slice_add_fusion.6
  295.4 1.2 collective-permute-done.18
  296.6 1.5 collective-permute-start.19
  298.1 2.3 collective-permute-done.19
  300.4 1.5 collective-permute-start.20
  301.9 2.3 collective-permute-done.20
  304.1 2.4 collective-permute-start.21
  306.5 2.2 collective-permute-done.21
  308.9 0.6 reshape.11
  309.6 0.7 copy.16
  (54 shorter events, 2.1 us)
Async XLA Ops:
  7.2 167.8 %all-gather.7.cloned.1.call-start = ((), (), s32[]{:S(2)}) async-start(), calls=%async_computation.1 | async-start | bytes 2359296 | tf_op jit(solution)/shard_map/all_gather | solution.py:444
  26.2 3.7 %collective-permute-start = (f32[2688,128]{1,0:T(8,128)}, f32[2688,128]{1,0:T(8,128)}, u32[]{:S(2)}, u32[]{:S(2)}) collective-permute-start(f32[2688,128]{1,0:T(8,128)} %get-tuple-element.11), channel_id=1, source_target_pairs={{0,2},{2,0},{4,6},{6,4},{8,10},{10,8},{12,14},{14,12},{16,18},{18,... | collective-permute-start | bytes 4128776 | tf_op jit(solution)/shard_map/ppermute | solution.py:361
  31.5 11.3 %collective-permute-start.7 = (f32[672,128]{1,0:T(8,128)S(1)}, f32[672,128]{1,0:T(8,128)S(1)}, u32[]{:S(2)}, u32[]{:S(2)}) collective-permute-start(f32[672,128]{1,0:T(8,128)S(1)} %constant_dynamic-slice_fusion.4), channel_id=1, source_target_pairs={{0,8},{2,10},{4,12},{6,14},{8,0},{10,2},{12,4},{14,6},{16,24},{18,... | collective-permute-start | bytes 1032200 | tf_op jit(solution)/shard_map/ppermute | solution.py:361
  34.5 11.2 %collective-permute-start.1 = (f32[672,128]{1,0:T(8,128)S(1)}, f32[672,128]{1,0:T(8,128)S(1)}, u32[]{:S(2)}, u32[]{:S(2)}) collective-permute-start(f32[672,128]{1,0:T(8,128)S(1)} %constant_dynamic-slice_fusion.7), channel_id=1, source_target_pairs={{0,4},{2,6},{4,0},{6,2},{8,12},{10,14},{12,8},{14,10},{16,20},{18,... | collective-permute-start | bytes 1032200 | tf_op jit(solution)/shard_map/ppermute | solution.py:361
  42.9 10.7 %collective-permute-start.8 = (f32[336,128]{1,0:T(8,128)S(1)}, f32[336,128]{1,0:T(8,128)S(1)}, u32[]{:S(2)}, u32[]{:S(2)}) collective-permute-start(f32[336,128]{1,0:T(8,128)S(1)} %constant_dynamic-slice_fusion.3), channel_id=1, source_target_pairs={{0,16},{2,18},{4,20},{6,22},{8,24},{10,26},{12,28},{14,30},{16,0},... | collective-permute-start | bytes 516104 | tf_op jit(solution)/shard_map/ppermute | solution.py:361
  45.8 9.2 %collective-permute-start.2 = (f32[336,128]{1,0:T(8,128)S(1)}, f32[336,128]{1,0:T(8,128)S(1)}, u32[]{:S(2)}, u32[]{:S(2)}) collective-permute-start(f32[336,128]{1,0:T(8,128)S(1)} %constant_dynamic-slice_fusion.6), channel_id=1, source_target_pairs={{0,8},{2,10},{4,12},{6,14},{8,0},{10,2},{12,4},{14,6},{16,24},{18,... | collective-permute-start | bytes 516104 | tf_op jit(solution)/shard_map/ppermute | solution.py:361
  53.6 4.6 %collective-permute-start.9 = (f32[168,128]{1,0:T(8,128)S(1)}, f32[168,128]{1,0:T(8,128)S(1)}, u32[]{:S(2)}, u32[]{:S(2)}) collective-permute-start(f32[168,128]{1,0:T(8,128)S(1)} %constant_dynamic-slice_fusion.2), channel_id=1, source_target_pairs={{0,4},{2,6},{4,0},{6,2},{8,12},{10,14},{12,8},{14,10},{16,20},{18,... | collective-permute-start | bytes 258056 | tf_op jit(solution)/shard_map/ppermute | solution.py:361
  55.1 7.4 %collective-permute-start.3 = (f32[168,128]{1,0:T(8,128)S(1)}, f32[168,128]{1,0:T(8,128)S(1)}, u32[]{:S(2)}, u32[]{:S(2)}) collective-permute-start(f32[168,128]{1,0:T(8,128)S(1)} %constant_dynamic-slice_fusion.5), channel_id=1, source_target_pairs={{0,16},{2,18},{4,20},{6,22},{8,24},{10,26},{12,28},{14,30},{16,0},... | collective-permute-start | bytes 258056 | tf_op jit(solution)/shard_map/ppermute | solution.py:361
  58.1 4.6 %collective-permute-start.10 = (f32[168,128]{1,0:T(8,128)S(1)}, f32[168,128]{1,0:T(8,128)S(1)}, u32[]{:S(2)}, u32[]{:S(2)}) collective-permute-start(f32[168,128]{1,0:T(8,128)S(1)} %dynamic-slice_add_fusion.4), channel_id=1, source_target_pairs={{0,4},{2,6},{4,0},{6,2},{8,12},{10,14},{12,8},{14,10},{16,20},{18,... | collective-permute-start | bytes 258056 | tf_op jit(solution)/shard_map/ppermute | solution.py:361
  62.5 9.4 %collective-permute-start.4 = (f32[168,128]{1,0:T(8,128)S(1)}, f32[168,128]{1,0:T(8,128)S(1)}, u32[]{:S(2)}, u32[]{:S(2)}) collective-permute-start(f32[168,128]{1,0:T(8,128)S(1)} %dynamic-slice_add_fusion.5), channel_id=1, source_target_pairs={{0,16},{2,18},{4,20},{6,22},{8,24},{10,26},{12,28},{14,30},{16,0},... | collective-permute-start | bytes 258056 | tf_op jit(solution)/shard_map/ppermute | solution.py:361
  62.7 11.0 %collective-permute-start.11 = (f32[336,128]{1,0:T(8,128)S(1)}, f32[336,128]{1,0:T(8,128)S(1)}, u32[]{:S(2)}, u32[]{:S(2)}) collective-permute-start(f32[336,128]{1,0:T(8,128)S(1)} %pad_maximum_fusion.6), channel_id=1, source_target_pairs={{0,16},{2,18},{4,20},{6,22},{8,24},{10,26},{12,28},{14,30},{16,0},... | collective-permute-start | bytes 516104 | tf_op jit(solution)/shard_map/ppermute | solution.py:361
  71.9 7.4 %collective-permute-start.5 = (f32[336,128]{1,0:T(8,128)S(1)}, f32[336,128]{1,0:T(8,128)S(1)}, u32[]{:S(2)}, u32[]{:S(2)}) collective-permute-start(f32[336,128]{1,0:T(8,128)S(1)} %pad_maximum_fusion.5), channel_id=1, source_target_pairs={{0,8},{2,10},{4,12},{6,14},{8,0},{10,2},{12,4},{14,6},{16,24},{18,... | collective-permute-start | bytes 516104 | tf_op jit(solution)/shard_map/ppermute | solution.py:361
  73.8 9.5 %collective-permute-start.12 = (f32[672,128]{1,0:T(8,128)S(1)}, f32[672,128]{1,0:T(8,128)S(1)}, u32[]{:S(2)}, u32[]{:S(2)}) collective-permute-start(f32[672,128]{1,0:T(8,128)S(1)} %pad_maximum_fusion.3), channel_id=1, source_target_pairs={{0,8},{2,10},{4,12},{6,14},{8,0},{10,2},{12,4},{14,6},{16,24},{18,... | collective-permute-start | bytes 1032200 | tf_op jit(solution)/shard_map/ppermute | solution.py:361
  79.4 7.3 %collective-permute-start.6 = (f32[672,128]{1,0:T(8,128)S(1)}, f32[672,128]{1,0:T(8,128)S(1)}, u32[]{:S(2)}, u32[]{:S(2)}) collective-permute-start(f32[672,128]{1,0:T(8,128)S(1)} %pad_maximum_fusion.2), channel_id=1, source_target_pairs={{0,4},{2,6},{4,0},{6,2},{8,12},{10,14},{12,8},{14,10},{16,20},{18,... | collective-permute-start | bytes 1032200 | tf_op jit(solution)/shard_map/ppermute | solution.py:361
  83.3 3.6 %copy-start.2 = (s32[5]{0:T(128)S(1)}, s32[5]{0:T(128)}, u32[]{:S(2)}) copy-start(s32[5]{0:T(128)} %param.5) | copy-start | bytes 64
  83.4 4.1 %collective-permute-start.14 = (f32[1344,128]{1,0:T(8,128)S(1)}, f32[1344,128]{1,0:T(8,128)S(1)}, u32[]{:S(2)}, u32[]{:S(2)}) collective-permute-start(f32[1344,128]{1,0:T(8,128)S(1)} %pad_maximum_fusion.1.near_b), channel_id=1, source_target_pairs={{0,2},{2,0},{4,6},{6,4},{8,10},{10,8},{12,14},{14,12},{16,18},{18,... | collective-permute-start | bytes 2064392 | tf_op jit(solution)/shard_map/ppermute | solution.py:361
  86.8 2.3 collective-permute-start.13
  147.7 7.2 %copy-start = (f32[8,1024]{1,0:T(8,128)}, f32[8,1024]{1,0:T(8,128)S(1)}, u32[]{:S(2)}) copy-start(f32[8,1024]{1,0:T(8,128)S(1)} %get-tuple-element.13.mean_ref) | copy-start | bytes 98308
  147.7 5.6 %collective-permute-start.15 = (bf16[64,1024]{1,0:T(8,128)(2,1)S(1)}, bf16[64,1024]{1,0:T(8,128)(2,1)S(1)}, u32[]{:S(2)}, u32[]{:S(2)}) collective-permute-start(bf16[64,1024]{1,0:T(8,128)(2,1)S(1)} %get-tuple-element.12), channel_id=1, source_target_pairs={{0,1},{1,0},{2,3},{3,2},{4,5},{5,4},{6,7},{7,6},{8,9},{9,8},{10,11... | collective-permute-start | bytes 393224 | tf_op jit(solution)/shard_map/ppermute | solution.py:440
  154.1 126.5 %all-gather.5.cloned.1.call-start = ((), (), s32[]{:S(2)}) async-start(), calls=%async_computation | async-start | bytes 12582912 | tf_op jit(solution)/shard_map/all_gather | solution.py:430
  154.9 4.0 %collective-permute-start.16 = (f32[8,1024]{1,0:T(8,128)S(1)}, f32[8,1024]{1,0:T(8,128)S(1)}, u32[]{:S(2)}, u32[]{:S(2)}) collective-permute-start(f32[8,1024]{1,0:T(8,128)S(1)} %get-tuple-element.13.mean_ref), channel_id=1, source_target_pairs={{0,1},{1,0},{2,3},{3,2},{4,5},{5,4},{6,7},{7,6},{8,9},{9,8},{10,11... | collective-permute-start | bytes 98312 | tf_op jit(solution)/shard_map/ppermute | solution.py:441
  158.9 121.8 %copy-start.1 = (f32[8,1024]{1,0:T(8,128)}, f32[8,1024]{1,0:T(8,128)S(1)}, u32[]{:S(2)}) copy-start(f32[8,1024]{1,0:T(8,128)S(1)} %collective-permute-done.16.far_mean_ref) | copy-start | bytes 98308
  291.0 3.7 %collective-permute-start.17 = (f32[32,128]{1,0:T(8,128)S(1)}, f32[32,128]{1,0:T(8,128)S(1)}, u32[]{:S(2)}, u32[]{:S(2)}) collective-permute-start(f32[32,128]{1,0:T(8,128)S(1)} %constant_dynamic-slice_fusion), channel_id=1, source_target_pairs={{0,1},{1,0},{2,3},{3,2},{4,5},{5,4},{6,7},{7,6},{8,9},{9,8},{10,11... | collective-permute-start | bytes 49160 | tf_op jit(solution)/shard_map/ppermute | solution.py:449
  295.4 1.2 collective-permute-start.18
  296.6 3.7 %collective-permute-start.19 = (f32[32,128]{1,0:T(8,128)S(1)}, f32[32,128]{1,0:T(8,128)S(1)}, u32[]{:S(2)}, u32[]{:S(2)}) collective-permute-start(f32[32,128]{1,0:T(8,128)S(1)} %add.119), channel_id=1, source_target_pairs={{0,4},{2,6},{4,0},{6,2},{8,12},{10,14},{12,8},{14,10},{16,20},{18,... | collective-permute-start | bytes 49160 | tf_op jit(solution)/shard_map/ppermute | solution.py:361
  300.4 3.7 %collective-permute-start.20 = (f32[32,128]{1,0:T(8,128)S(1)}, f32[32,128]{1,0:T(8,128)S(1)}, u32[]{:S(2)}, u32[]{:S(2)}) collective-permute-start(f32[32,128]{1,0:T(8,128)S(1)} %add.120), channel_id=1, source_target_pairs={{0,8},{2,10},{4,12},{6,14},{8,0},{10,2},{12,4},{14,6},{16,24},{18,... | collective-permute-start | bytes 49160 | tf_op jit(solution)/shard_map/ppermute | solution.py:361
  304.1 4.6 %collective-permute-start.21 = (f32[32,128]{1,0:T(8,128)S(1)}, f32[32,128]{1,0:T(8,128)S(1)}, u32[]{:S(2)}, u32[]{:S(2)}) collective-permute-start(f32[32,128]{1,0:T(8,128)S(1)} %add.121), channel_id=1, source_target_pairs={{0,16},{2,18},{4,20},{6,22},{8,24},{10,26},{12,28},{14,30},{16,0},... | collective-permute-start | bytes 49160 | tf_op jit(solution)/shard_map/ppermute | solution.py:361
Sparse Core Ops, SparseCore 0:
  154.2 20.6 all-gather.6
  176.5 104.1 all-gather.4

commit v2 on v1

--- a/solution.py
+++ b/solution.py
@@ -10,6 +10,7 @@
 BLK = 128
 SUB = 8
 GROUP = 8
+CHUNKS = 6
 HI = lax.Precision.HIGHEST
 NT = (((1,), (1,)), ((), ()))
 TN = (((0,), (0,)), ((), ()))
@@ -66,12 +67,6 @@
 
 def drop(x, row):
     return jnp.broadcast_to(x[row:row + 1, :], (SUB, BLK))
-
-
-def total_of(terms):
-    while len(terms) > 1:
-        terms = [sum(terms[i:i + 2][1:], terms[i]) for i in range(0, len(terms), 2)]
-    return terms[0]
 
 
 def solve_pivots(cols, right, rows_at):
@@ -112,17 +107,25 @@
             if i == k:
                 fresh.append(right)
             else:
-                change = total_of([spread(strips[i], at + j) * tops[j] for j in range(SUB)])
-                fresh.append(jnp.where(inside, 0.0, strips[i]) - change)
+                rest = jnp.where(inside, 0.0, strips[i])
+                for j in range(SUB):
+                    rest = rest - spread(strips[i], at + j) * tops[j]
+                fresh.append(rest)
         strips = fresh
     return jnp.concatenate(strips, axis=0)
 
 
-def gram_kernel(ntraits, rank_ref, geno_ref, traits_ref, near_ref, away_ref, sent_ref, kept_ref, side, *panels):
+def piece_starts(rows):
+    each = rows * 7 // 64
+    return [each * i for i in range(CHUNKS + 1)] + [rows]
+
+
+def gram_kernel(ntraits, rank_ref, geno_ref, traits_ref, near_ref, away_ref, kept_ref, *refs):
     nvars = geno_ref.shape[1]
     step = pl.program_id(0)
     half = pl.num_programs(0) // 2
     wide = 2 * BLK
+    pieces, side, panels = refs[:CHUNKS + 1], refs[CHUNKS + 1], refs[CHUNKS + 2:]
 
     @pl.when(step == 0)
     def _():
@@ -132,9 +135,15 @@
 
     dosage = geno_ref[...].astype(jnp.float32).astype(jnp.bfloat16)
 
-    @pl.when(step < half)
-    def _():
-        sent_ref[...] = dosage
+    count = dosage.shape[0]
+    for tile in range(piece_starts(geno_ref.shape[0] * 2)[-1] // count):
+        @pl.when(step == tile)
+        def _(tile=tile):
+            starts = piece_starts(count * 2)
+            for piece, first, end in zip(pieces, starts, starts[1:]):
+                low, high = max(first, tile * count), min(end, (tile + 1) * count)
+                if low < high:
+                    piece[low - first:high - first, :] = dosage[low - tile * count:high - tile * count, :]
 
     @pl.when(step >= half)
     def _():
@@ -198,7 +207,8 @@
     def source(i, place_ref):
         return (lax.rem(i + half * (1 - place_ref[0]), steps), 0)
 
-    halves = jax.ShapeDtypeStruct((count // 2, nvars), jnp.bfloat16)
+    starts = piece_starts(count // 2)
+    sizes = [end - first for first, end in zip(starts, starts[1:])]
     return pl.pallas_call(
         functools.partial(gram_kernel, ntraits),
         grid_spec=pltpu.PrefetchScalarGridSpec(
@@ -208,13 +218,14 @@
             out_specs=[
                 pl.BlockSpec((total // 2, BLK), lambda i, rank_ref: (0, 0)),
                 pl.BlockSpec((total // 2, BLK), lambda i, rank_ref: (0, 0)),
-                pl.BlockSpec((tile, nvars), lambda i, rank_ref: (jnp.minimum(i, half - 1), 0)),
                 pl.BlockSpec((tile, nvars), lambda i, rank_ref: (jnp.maximum(i - half, 0), 0)),
-            ],
+            ]
+            + [pl.BlockSpec((size, nvars), lambda i, rank_ref: (0, 0)) for size in sizes],
             scratch_shapes=[pltpu.VMEM((side_rows(ntraits), nvars), jnp.float32)]
             + [pltpu.VMEM((nvars - 2 * BLK * j, 2 * BLK), jnp.float32) for j in range(nvars // (2 * BLK))],
         ),
-        out_shape=[jax.ShapeDtypeStruct((total // 2, BLK), jnp.float32)] * 2 + [halves, halves],
+        out_shape=[jax.ShapeDtypeStruct((total // 2, BLK), jnp.float32)] * 2
+        + [jax.ShapeDtypeStruct((size, nvars), jnp.bfloat16) for size in [count // 2] + sizes],
         compiler_params=pltpu.CompilerParams(vmem_limit_bytes=48 * 1024 * 1024),
         name="gram_sums",
     )(place, genotypes, traits)
@@ -294,24 +305,25 @@
             pltpu.VMEM((nvars + ntraits, nvars), jnp.float32),
         ],
         compiler_params=pltpu.CompilerParams(vmem_limit_bytes=48 * 1024 * 1024),
-        cost_estimate=pl.CostEstimate(flops=10**6, bytes_accessed=10**6, transcendentals=0),
+        cost_estimate=pl.CostEstimate(flops=46 * 10**9, bytes_accessed=10**6, transcendentals=0),
         name="ridge_solve",
     )(lam, *pieces)
 
 
-def level_kernel(npen, own_ref, halves_ref, coef_ref, mean_ref, far_mean_ref, traits_ref, out_ref, pred, other_ref, sem):
+def level_kernel(npen, own_ref, coef_ref, mean_ref, far_mean_ref, traits_ref, *refs):
     rank = lax.axis_index("blk")
     ntraits = coef_ref.shape[2]
     nvars = own_ref.shape[1]
     count = own_ref.shape[0]
     stack = 2 * npen
     tile = 512
-    fetch = pltpu.make_async_copy(halves_ref.at[1 - rank], other_ref, sem)
-    fetch.start()
+    pieces, (out_ref, pred, other_ref) = refs[:-3], refs[-3:]
+    low = 0
+    for piece in pieces:
+        other_ref[low:low + piece.shape[0], :] = piece[...]
+        low += piece.shape[0]
     for place in range(2):
         block = rank if place == 0 else 1 - rank
-        if place == 1:
-            fetch.wait()
         source = own_ref if place == 0 else other_ref
         mean = (mean_ref if place == 0 else far_mean_ref)[0:1, :]
         coef = jnp.concatenate([coef_ref[r, block] for r in range(npen)], axis=0)
@@ -338,23 +350,22 @@
         out_ref[t:t + SUB, :] = acc
 
 
-def level_sums(own, halves, coefs, mean, far_mean, traits, npen):
+def level_sums(own, others, coefs, mean, far_mean, traits, npen):
     ntraits = traits.shape[1]
     count = own.shape[0]
     vmem = pl.BlockSpec(memory_space=pltpu.VMEM)
     return pl.pallas_call(
         functools.partial(level_kernel, npen),
         out_shape=jax.ShapeDtypeStruct((ntraits, BLK), jnp.float32),
-        in_specs=[vmem, pl.BlockSpec(memory_space=pl.ANY)] + [vmem] * 4,
+        in_specs=[vmem] * (5 + len(others)),
         out_specs=pl.BlockSpec(memory_space=pltpu.VMEM),
         scratch_shapes=[
             pltpu.VMEM(((2 * npen + 1) * ntraits, count), jnp.float32),
             pltpu.VMEM(own.shape, own.dtype),
-            pltpu.SemaphoreType.DMA,
         ],
         compiler_params=pltpu.CompilerParams(vmem_limit_bytes=56 * 1024 * 1024),
         name="level_sums",
-    )(own, halves, coefs, mean, far_mean, traits)
+    )(own, coefs, mean, far_mean, traits, *others)
 
 
 def swapped(x, bit):
@@ -365,31 +376,78 @@
     return lax.rem(lax.div(lax.axis_index("samp"), 1 << bit), 2)
 
 
-def halved(x, bit):
+def add_kernel(near_a, far_a, near_b, far_b, *refs):
+    out_a, out_b = refs[-2:]
+    out_a[...] = near_a[...] + far_a[...]
+    out_b[...] = near_b[...] + far_b[...]
+
+
+def join_kernel(bits, near_a, far_a, near_b, far_b, *refs):
+    rank = lax.axis_index("samp")
+    for bit, near, far, out in zip(bits, (near_a, near_b), (far_a, far_b), refs[-2:]):
+        rows = near.shape[0]
+        mine = lax.rem(lax.div(rank, 1 << bit), 2)
+        out[pl.ds(pl.multiple_of(mine * rows, SUB), rows), :] = near[...]
+        out[pl.ds(pl.multiple_of((1 - mine) * rows, SUB), rows), :] = far[...]
+
+
+def step_call(kernel, near, far, arrived, grow, name):
+    operands = [near[0], far[0], near[1], far[1]] + arrived
+    return pl.pallas_call(
+        kernel,
+        out_shape=[jax.ShapeDtypeStruct((grow * x.shape[0], x.shape[1]), x.dtype) for x in near],
+        in_specs=[pl.BlockSpec(memory_space=pltpu.VMEM)] * 4 + [pl.BlockSpec(memory_space=pl.ANY)] * len(arrived),
+        out_specs=[pl.BlockSpec(memory_space=pltpu.VMEM)] * 2,
+        cost_estimate=pl.CostEstimate(flops=10**6, bytes_accessed=10**6, transcendentals=0),
+        name=name,
+    )(*operands)
+
+
+def pass_kernel(coef_ref, piece_ref, out_ref):
+    out_ref[...] = coef_ref[...]
+
+
+def after(coef, piece):
+    return pl.pallas_call(
+        pass_kernel,
+        out_shape=jax.ShapeDtypeStruct(coef.shape, coef.dtype),
+        in_specs=[pl.BlockSpec(memory_space=pltpu.VMEM), pl.BlockSpec(memory_space=pl.ANY)],
+        out_specs=pl.BlockSpec(memory_space=pltpu.VMEM),
+        cost_estimate=pl.CostEstimate(flops=10**6, bytes_accessed=10**5, transcendentals=0),
+        name="after_piece",
+    )(coef, piece)
+
+
+def cut(x, bit):
     rows = x.shape[0] // 2
     mine = place_bit(bit)
-    far = swapped(lax.dynamic_slice_in_dim(x, (1 - mine) * rows, rows, 0), bit)
-    return lax.dynamic_slice_in_dim(x, mine * rows, rows, 0) + far
-
-
-def doubled(x, bit):
-    far = swapped(x, bit)
-    even = place_bit(bit) == 0
-    return jnp.concatenate([jnp.where(even, x, far), jnp.where(even, far, x)], axis=0)
-
-
-def all_sums(x, away):
+    return lax.dynamic_slice_in_dim(x, mine * rows, rows, 0), lax.dynamic_slice_in_dim(x, (1 - mine) * rows, rows, 0)
+
+
+def all_sums(x, away, riders):
     bits = list(range(1, lax.axis_size("samp").bit_length() - 1))
+    orders = (bits, bits[1:] + bits[:1])
+    brought = []
+
+    def ride():
+        if len(brought) < len(riders):
+            brought.append(riders[len(brought)]())
+            return [brought[-1]]
+        return []
+
     x = x + swapped(away, 0)
     rows = x.shape[0] // 2
-    near = []
-    for part, order in ((x[:rows], bits), (x[rows:], bits[1:] + bits[:1])):
-        for bit in order:
-            part = halved(part, bit)
-        for bit in reversed(order):
-            part = doubled(part, bit)
-        near.append(part)
-    return near + [swapped(part, 0) for part in near]
+    parts = [x[:rows], x[rows:]]
+    for pair in zip(*orders):
+        arrived = ride()
+        kept, sent = zip(*[cut(part, bit) for part, bit in zip(parts, pair)])
+        far = [swapped(part, bit) for part, bit in zip(sent, pair)]
+        parts = step_call(add_kernel, kept, far, arrived, 1, "step_add")
+    for pair in reversed(list(zip(*orders))):
+        arrived = ride()
+        far = [swapped(part, bit) for part, bit in zip(parts, pair)]
+        parts = step_call(functools.partial(join_kernel, pair), parts, far, arrived, 2, "step_join")
+    return list(parts) + [swapped(part, 0) for part in parts], brought
 
 
 def small_sum(x):
@@ -425,10 +483,10 @@
     blk_rank = lax.axis_index("blk")
     paired = nblk == 2
     place = jnp.stack([blk_rank if paired else jnp.int32(0), place_bit(0)])
-    near, away, sent, kept = gram(genotypes, traits, place, members)
-    if paired:
-        halves = lax.all_gather(sent, "blk")
-    pieces = all_sums(near, away)
+    near, away, kept, *sent = gram(genotypes, traits, place, members)
+    riders = [functools.partial(lax.ppermute, piece, "blk", [(0, 1), (1, 0)]) for piece in sent] if paired else []
+    pieces, others = all_sums(near, away, riders[:CHUNKS])
+    others += [rider() for rider in riders[len(others):]]
     lam = nsamp * jnp.exp2((penalty_index.astype(jnp.float32) - 8.0) / 2.0)
     mine = lax.dynamic_index_in_dim(lam, (samp_rank % GROUP) % npen, 0, keepdims=True).reshape(1, 1)
     coef, mean = solve(pieces, mine, nsamp, nvars, ntraits)
@@ -437,13 +495,14 @@
         coefs = lax.all_gather(coef, "samp", axis_index_groups=groups)[:npen]
         dosage = genotypes.astype(jnp.bfloat16)
         return level_from_predictions(coefs, mean[0], dosage, traits, nvars)
+    coef = after(coef, others[-1])
     coef_far = lax.ppermute(coef, "blk", [(0, 1), (1, 0)])
     mean_far = lax.ppermute(mean, "blk", [(0, 1), (1, 0)])
     first = blk_rank == 0
     both = jnp.stack([jnp.where(first, coef, coef_far), jnp.where(first, coef_far, coef)])
     coefs = lax.all_gather(both, "samp", axis_index_groups=groups)
     rows = lax.dynamic_slice_in_dim(traits, blk_rank * (count // 2), count // 2, 0)
-    found = level_sums(kept, halves, coefs, mean, mean_far, rows, npen)
+    found = level_sums(kept, others, coefs, mean, mean_far, rows, npen)
     stack = nblk * npen
     each = ntraits // nblk
     far = lax.ppermute(lax.dynamic_slice_in_dim(found, (1 - blk_rank) * each, each, 0), "blk", [(0, 1), (1, 0)])

time: 321 us -> 246 us (0.77)
  waiting for transfers between devices: 183 us -> 63.4 us
  local copies, waits for them, and re-layouts: 5.4 us -> 22.6 us
  starting transfers between devices: 25.7 us -> 39.5 us
  Pallas kernels: 85.5 us -> 98.4 us
    all_gather x1 -> x0, waiting for transfers between devices: 106 us -> none  [local(): halves = lax.all_gather(sent, 'blk')]
    pallas_call x0 -> x7, Pallas kernels: none -> 13.8 us  [the longest x6 12.2 us: step_call(): pl.pallas_call(kernel, out_shape=[jax.ShapeDtypeStruct((grow * x.shape[0]...]
    ppermute x19, waiting for transfers between devices: 51.2 us -> 38.4 us  [swapped(): lax.ppermute(x, 'samp', [(i, i ^ 1 << bit) for i in range(lax.axis_size('...]
    ppermute x0 -> x7, starting transfers between devices: none -> 10.4 us  [the longest x6 8.91 us: ride(): brought.append(riders[len(brought)]())]
    unnamed x8 -> x52, local copies, waits for them, and re-layouts: 2.21 us -> 11.1 us
    dynamic_slice x6, local copies, waits for them, and re-layouts: 0.13 us -> 8.36 us  [cut(): lax.dynamic_slice_in_dim(x, (1 - mine) * rows, rows, 0)]
  transfers between devices with their start and end apart: 24 -> 30, of which waited for: 21 -> 21; matrix products, arithmetic and copies ran while one was open for 1% -> 5% of each run, Pallas kernels for 0% -> 28%
where the time goes in v2:
time: 246 us; the launch traced here: 242 us
  Pallas kernels  98.4 us (40%)
  waiting for transfers between devices  63.4 us (26%)
  starting transfers between devices  39.5 us (16%)
  local copies, waits for them, and re-layouts  22.6 us (9%)
  between operations  14.4 us (6%)
  other arithmetic  3.96 us (2%)
    pallas_call x1, Pallas kernels, solve(): pl.pallas_call(functools.partial(solve_kernel, nsamp, ntraits), out_shape...  57.5 us
    ppermute x19, waiting for transfers between devices, swapped(): lax.ppermute(x, 'samp', [(i, i ^ 1 << bit) for i in range(lax.axis_size('...  38.4 us
    ppermute x19, starting transfers between devices, swapped(): lax.ppermute(x, 'samp', [(i, i ^ 1 << bit) for i in range(lax.axis_size('...  24.3 us
    pallas_call x1, Pallas kernels, gram(): pl.pallas_call(functools.partial(gram_kernel, ntraits), grid_spec=pltpu.P...  17.1 us
    all_gather x1, waiting for transfers between devices, local(): coefs = lax.all_gather(both, 'samp', axis_index_groups=groups)  15.3 us
    pallas_call x6, Pallas kernels, step_call(): pl.pallas_call(kernel, out_shape=[jax.ShapeDtypeStruct((grow * x.shape[0]...  12.2 us
    unnamed x52, local copies, waits for them, and re-layouts  11.1 us
    pallas_call x1, Pallas kernels, level_sums(): pl.pallas_call(functools.partial(level_kernel, npen), out_shape=jax.Shape...  10 us
  transfers between devices with their start and end apart: 30, of which 21 were waited for; matrix products, arithmetic and copies ran while one was open for 5% of the time, Pallas kernels for 28%

profile of v2, /device:TPU:0, one launch (start us, length us, event | category | flops | bytes accessed | tf_op | source)
XLA Modules:
  0.0 242.2 jit_solution(10200944273754142091)
XLA Ops:
  7.2 1.5 copy.13.traits_ref
  8.8 17.1 %gram_sums.1 = (f32[2688,128]{1,0:T(8,128)S(1)}, f32[2688,128]{1,0:T(8,128)}, bf16[2048,1024]{1,0:T(8,128)(2,1)}, bf16[224,1024]{1,0:T(8,128)(2,1)}, bf16[224,10...) custom-call(s32[2]{0:T(128)S(1)} %pad_add_fusion.rank_ref, ...), custom_call_target="tpu_custom_call" | custom-call | tf_op jit(solution)/shard_map/gram_sums/pallas_call | solution.py:212
  28.8 2.4 collective-permute-start.3
  34.3 2.8 %collective-permute-start.2 = (f32[672,128]{1,0:T(8,128)S(1)}, f32[672,128]{1,0:T(8,128)S(1)}, u32[]{:S(2)}, u32[]{:S(2)}) collective-permute-start(f32[672,128]{1,0:T(8,128)S(1)} %get-tuple-element.58), channel_id=1, source_target_pairs={{0,8},{2,10},{4,12},{6,14},{8,0},{10,2},{12,4},{14,6},{16,24},{18,... | collective-permute-start | bytes 1032200 | tf_op jit(solution)/shard_map/ppermute | solution.py:372
  38.0 1.5 collective-permute-start.1
  41.0 1.8 collective-permute-done.3.refs_0_
  42.9 2.6 %collective-permute-done.2.far_b = f32[672,128]{1,0:T(8,128)S(1)} collective-permute-done((f32[672,128]{1,0:T(8,128)S(1)}, f32[672,128]{1,0:T(8,128)S(1)}, u32[]{:S(2)}, u32[]{:S(2)}) %collective-permute-start.2) | collective-permute-done | bytes 344096 | tf_op jit(solution)/shard_map/ppermute | solution.py:372
  45.5 2.6 %collective-permute-done.1.far_a = f32[672,128]{1,0:T(8,128)S(1)} collective-permute-done((f32[672,128]{1,0:T(8,128)}, f32[672,128]{1,0:T(8,128)S(1)}, u32[]{:S(2)}, u32[]{:S(2)}) %collective-permute-start.1) | collective-permute-done | bytes 344096 | tf_op jit(solution)/shard_map/ppermute | solution.py:372
  48.8 2.3 step_add.3
  51.1 1.8 constant_dynamic-slice_fusion.8
  53.1 1.8 constant_dynamic-slice_fusion.6
  54.9 2.8 %collective-permute-start.5 = (f32[336,128]{1,0:T(8,128)}, f32[336,128]{1,0:T(8,128)}, u32[]{:S(2)}, u32[]{:S(2)}) collective-permute-start(f32[336,128]{1,0:T(8,128)} %get-tuple-element.62), channel_id=1, source_target_pairs={{0,16},{2,18},{4,20},{6,22},{8,24},{10,26},{12,28},{14,30},{16,0},... | collective-permute-start | bytes 516104 | tf_op jit(solution)/shard_map/ppermute | solution.py:372
  57.7 1.5 collective-permute-start.9
  59.7 1.5 collective-permute-start.15
  61.2 4.0 %collective-permute-done.5.far_b = f32[336,128]{1,0:T(8,128)} collective-permute-done((f32[336,128]{1,0:T(8,128)}, f32[336,128]{1,0:T(8,128)}, u32[]{:S(2)}, u32[]{:S(2)}) %collective-permute-start.5) | collective-permute-done | bytes 172064 | tf_op jit(solution)/shard_map/ppermute | solution.py:372
  65.2 1.9 step_add.4
  67.2 1.6 constant_dynamic-slice_fusion.4
  68.7 1.6 constant_dynamic-slice_fusion.2
  71.7 3.8 %collective-permute-done.7.far_a = f32[168,128]{1,0:T(8,128)S(1)} collective-permute-done((f32[168,128]{1,0:T(8,128)S(1)}, f32[168,128]{1,0:T(8,128)S(1)}, u32[]{:S(2)}, u32[]{:S(2)}) %collective-permute-start.7) | collective-permute-done | bytes 86048 | tf_op jit(solution)/shard_map/ppermute | solution.py:372
  76.1 1.7 step_add.5
  77.8 2.2 collective-permute-start.10
  81.5 2.9 %collective-permute-done.10.far_a = f32[168,128]{1,0:T(8,128)S(1)} collective-permute-done((f32[168,128]{1,0:T(8,128)}, f32[168,128]{1,0:T(8,128)S(1)}, u32[]{:S(2)}, u32[]{:S(2)}) %collective-permute-start.10) | collective-permute-done | bytes 86048 | tf_op jit(solution)/shard_map/ppermute | solution.py:372
  85.6 1.8 step_join.3
  87.4 2.3 collective-permute-start.13
  91.0 1.5 collective-permute-start.18
  92.5 2.5 %collective-permute-done.13.far_a = f32[336,128]{1,0:T(8,128)S(1)} collective-permute-done((f32[336,128]{1,0:T(8,128)}, f32[336,128]{1,0:T(8,128)S(1)}, u32[]{:S(2)}, u32[]{:S(2)}) %collective-permute-start.13) | collective-permute-done | bytes 172064 | tf_op jit(solution)/shard_map/ppermute | solution.py:372
  95.1 3.1 %collective-permute-done.14.far_b = f32[336,128]{1,0:T(8,128)S(1)} collective-permute-done((f32[336,128]{1,0:T(8,128)}, f32[336,128]{1,0:T(8,128)S(1)}, u32[]{:S(2)}, u32[]{:S(2)}) %collective-permute-start.14) | collective-permute-done | bytes 172064 | tf_op jit(solution)/shard_map/ppermute | solution.py:372
  98.9 2.1 step_join.4
  100.9 1.5 collective-permute-start.16
  102.5 5.9 %collective-permute-done.16.far_a = f32[672,128]{1,0:T(8,128)S(1)} collective-permute-done((f32[672,128]{1,0:T(8,128)}, f32[672,128]{1,0:T(8,128)S(1)}, u32[]{:S(2)}, u32[]{:S(2)}) %collective-permute-start.16) | collective-permute-done | bytes 344096 | tf_op jit(solution)/shard_map/ppermute | solution.py:372
  108.4 1.5 collective-permute-done.17.far_b
  110.7 2.5 %step_join.5 = (f32[1344,128]{1,0:T(8,128)}, f32[1344,128]{1,0:T(8,128)}) custom-call(f32[672,128]{1,0:T(8,128)} %get-tuple-element.42.near_a, f32[672,128]{1,0:T(8,128)} %copy-done.14, f32[672,128]{1,0:T(8,128)} %get-tuple-element.43.near_b, f32[672,128]{1,0:T(8,128)} %copy-done.15, bf16[224,1024]{1,0:T(8,128)(2,1)} %copy-done.11), custom_call_target="tpu_custom_call" | custom-call | flops 1000000 | bytes 1000000 | tf_op jit(solution)/shard_map/step_join/pallas_call | solution.py:396
  113.7 1.5 collective-permute-start.21
  118.7 57.5 %ridge_solve.1 = (bf16[64,1024]{1,0:T(8,128)(2,1)S(1)}, f32[8,1024]{1,0:T(8,128)S(1)}) custom-call(f32[1,1]{1,0:T(1,128)} %bitcast.2.lam_ref, f32[1344,128]{1,0:T(8,128)S(1)} %copy-done.2, f32[1344,128]{1,0:T(8,128)S(1)} %copy-done.3, f32[1344,128]{1,0:T(8,128)S(1)} %collective-permute-done.19.far_a, f32[1344,128]{1,0:T(8,128)S(1)} %collective-permute-done.20.far_b), custom_call_target="tpu_custom_call" | custom-call | flops 46000001024 | bytes 1000000 | tf_op jit(solution)/shard_map/ridge_solve/pallas_call | solution.py:298
  176.8 1.6 after_piece.1
  178.4 1.5 collective-permute-start.22
  179.9 4.3 %collective-permute-done.22 = bf16[64,1024]{1,0:T(8,128)(2,1)S(1)} collective-permute-done((bf16[64,1024]{1,0:T(8,128)(2,1)}, bf16[64,1024]{1,0:T(8,128)(2,1)S(1)}, u32[]{:S(2)}, u32[]{:S(2)}) %collective-permute-start.22) | collective-permute-done | bytes 131104 | tf_op jit(solution)/shard_map/ppermute | solution.py:499
  185.9 1.6 collective-permute-start.23
  188.3 1.5 collective-permute-done.23.far_mean_ref
  189.9 15.3 %all-gather.3.cloned.1.call-done = bf16[16,64,1024]{2,1,0:T(8,128)(2,1)} async-done(((bf16[2,64,1024]{2,1,0:T(8,128)(2,1)}), bf16[16,64,1024]{2,1,0:T(8,128)(2,1)}) %all-gather.3.cloned.1.call-update) | async-done | bytes 2097168 | tf_op jit(solution)/shard_map/all_gather | solution.py:503
  205.2 10.0 %level_sums.1 = f32[64,128]{1,0:T(8,128)} custom-call(bf16[2048,1024]{1,0:T(8,128)(2,1)} %get-tuple-element.26.own_ref, bf16[8,2,64,1024]{3,2,1,0:T(8,128)(2,1)} %bitcast.11, f32[8,1024]{1,0:T(8,128)} %copy-done.1, f32[8,1024]{1,0:T(8,128)} %copy-done.23, bf16[2048,64]{1,0:T(8,128)(2,1)} %constant_dynamic-slice_fusion.1.traits_ref, ...), custom_call_target="tpu_custom_call" | custom-call | tf_op jit(solution)/shard_map/level_sums/pallas_call | solution.py:357
  215.9 1.6 collective-permute-start.24
  217.5 2.1 collective-permute-done.24
  223.0 2.2 collective-permute-done.26
  225.3 1.6 collective-permute-start.27
  226.9 2.2 collective-permute-done.27
  229.0 2.6 %collective-permute-start.28 = (f32[32,128]{1,0:T(8,128)S(1)}, f32[32,128]{1,0:T(8,128)S(1)}, u32[]{:S(2)}, u32[]{:S(2)}) collective-permute-start(f32[32,128]{1,0:T(8,128)S(1)} %add.97), channel_id=1, source_target_pairs={{0,16},{2,18},{4,20},{6,22},{8,24},{10,26},{12,28},{14,30},{16,0},... | collective-permute-start | bytes 49160 | tf_op jit(solution)/shard_map/ppermute | solution.py:372
  231.6 2.1 collective-permute-done.28
  (98 shorter events, 30.5 us)
Async XLA Ops:
  7.2 198.0 %all-gather.3.cloned.1.call-start = ((), (), s32[]{:S(2)}) async-start(), calls=%async_computation | async-start | bytes 2359296 | tf_op jit(solution)/shard_map/all_gather | solution.py:503
  25.9 0.8 copy-start.4
  26.7 0.8 copy-start.6
  27.5 0.8 copy-start.8
  28.2 3.6 %collective-permute-start = (f32[2688,128]{1,0:T(8,128)}, f32[2688,128]{1,0:T(8,128)}, u32[]{:S(2)}, u32[]{:S(2)}) collective-permute-start(f32[2688,128]{1,0:T(8,128)} %get-tuple-element.28), channel_id=1, source_target_pairs={{0,2},{2,0},{4,6},{6,4},{8,10},{10,8},{12,14},{14,12},{16,18},{18,... | collective-permute-start | bytes 4128776 | tf_op jit(solution)/shard_map/ppermute | solution.py:372
  28.8 14.1 %collective-permute-start.3 = (bf16[224,1024]{1,0:T(8,128)(2,1)}, bf16[224,1024]{1,0:T(8,128)(2,1)}, u32[]{:S(2)}, u32[]{:S(2)}) collective-permute-start(bf16[224,1024]{1,0:T(8,128)(2,1)} %get-tuple-element.29), channel_id=1, source_target_pairs={{0,1},{1,0},{2,3},{3,2},{4,5},{5,4},{6,7},{7,6},{8,9},{9,8},{10,11... | collective-permute-start | bytes 1376264 | tf_op jit(solution)/shard_map/ppermute | solution.py:434
  33.5 6.1 %copy-start.9 = (bf16[224,1024]{1,0:T(8,128)(2,1)S(1)}, bf16[224,1024]{1,0:T(8,128)(2,1)}, u32[]{:S(2)}) copy-start(bf16[224,1024]{1,0:T(8,128)(2,1)} %copy-done.8) | copy-start | bytes 1376260
  34.3 11.2 %collective-permute-start.2 = (f32[672,128]{1,0:T(8,128)S(1)}, f32[672,128]{1,0:T(8,128)S(1)}, u32[]{:S(2)}, u32[]{:S(2)}) collective-permute-start(f32[672,128]{1,0:T(8,128)S(1)} %get-tuple-element.58), channel_id=1, source_target_pairs={{0,8},{2,10},{4,12},{6,14},{8,0},{10,2},{12,4},{14,6},{16,24},{18,... | collective-permute-start | bytes 1032200 | tf_op jit(solution)/shard_map/ppermute | solution.py:372
  38.0 10.0 %collective-permute-start.1 = (f32[672,128]{1,0:T(8,128)}, f32[672,128]{1,0:T(8,128)S(1)}, u32[]{:S(2)}, u32[]{:S(2)}) collective-permute-start(f32[672,128]{1,0:T(8,128)} %get-tuple-element.60), channel_id=1, source_target_pairs={{0,4},{2,6},{4,0},{6,2},{8,12},{10,14},{12,8},{14,10},{16,20},{18,... | collective-permute-start | bytes 1032200 | tf_op jit(solution)/shard_map/ppermute | solution.py:372
  39.5 20.1 %collective-permute-start.6 = (bf16[224,1024]{1,0:T(8,128)(2,1)S(1)}, bf16[224,1024]{1,0:T(8,128)(2,1)}, u32[]{:S(2)}, u32[]{:S(2)}) collective-permute-start(bf16[224,1024]{1,0:T(8,128)(2,1)S(1)} %copy-done.9), channel_id=1, source_target_pairs={{0,1},{1,0},{2,3},{3,2},{4,5},{5,4},{6,7},{7,6},{8,9},{9,8},{10,11... | collective-permute-start | bytes 1376264 | tf_op jit(solution)/shard_map/ppermute | solution.py:434
  45.5 2.6 %copy-start.12 = (f32[672,128]{1,0:T(8,128)}, f32[672,128]{1,0:T(8,128)S(1)}, u32[]{:S(2)}) copy-start(f32[672,128]{1,0:T(8,128)S(1)} %collective-permute-done.2.far_b) | copy-start | bytes 1032196
  48.0 0.8 copy-start.13
  48.8 8.8 %copy-start.7 = (bf16[224,1024]{1,0:T(8,128)(2,1)S(1)}, bf16[224,1024]{1,0:T(8,128)(2,1)}, u32[]{:S(2)}) copy-start(bf16[224,1024]{1,0:T(8,128)(2,1)} %copy-done.6) | copy-start | bytes 1376260
  48.8 10.3 %copy-start.5 = (bf16[224,1024]{1,0:T(8,128)(2,1)S(1)}, bf16[224,1024]{1,0:T(8,128)(2,1)}, u32[]{:S(2)}) copy-start(bf16[224,1024]{1,0:T(8,128)(2,1)} %copy-done.4) | copy-start | bytes 1376260
  52.8 8.3 %collective-permute-start.4 = (f32[336,128]{1,0:T(8,128)}, f32[336,128]{1,0:T(8,128)S(1)}, u32[]{:S(2)}, u32[]{:S(2)}) collective-permute-start(f32[336,128]{1,0:T(8,128)} %get-tuple-element.64), channel_id=1, source_target_pairs={{0,8},{2,10},{4,12},{6,14},{8,0},{10,2},{12,4},{14,6},{16,24},{18,... | collective-permute-start | bytes 516104 | tf_op jit(solution)/shard_map/ppermute | solution.py:372
  54.9 10.3 %collective-permute-start.5 = (f32[336,128]{1,0:T(8,128)}, f32[336,128]{1,0:T(8,128)}, u32[]{:S(2)}, u32[]{:S(2)}) collective-permute-start(f32[336,128]{1,0:T(8,128)} %get-tuple-element.62), channel_id=1, source_target_pairs={{0,16},{2,18},{4,20},{6,22},{8,24},{10,26},{12,28},{14,30},{16,0},... | collective-permute-start | bytes 516104 | tf_op jit(solution)/shard_map/ppermute | solution.py:372
  57.7 14.1 %collective-permute-start.9 = (bf16[224,1024]{1,0:T(8,128)(2,1)S(1)}, bf16[224,1024]{1,0:T(8,128)(2,1)}, u32[]{:S(2)}, u32[]{:S(2)}) collective-permute-start(bf16[224,1024]{1,0:T(8,128)(2,1)S(1)} %copy-done.7), channel_id=1, source_target_pairs={{0,1},{1,0},{2,3},{3,2},{4,5},{5,4},{6,7},{7,6},{8,9},{9,8},{10,11... | collective-permute-start | bytes 1376264 | tf_op jit(solution)/shard_map/ppermute | solution.py:434
  59.2 22.3 %collective-permute-start.12 = (bf16[224,1024]{1,0:T(8,128)(2,1)S(1)}, bf16[224,1024]{1,0:T(8,128)(2,1)}, u32[]{:S(2)}, u32[]{:S(2)}) collective-permute-start(bf16[224,1024]{1,0:T(8,128)(2,1)S(1)} %copy-done.5), channel_id=1, source_target_pairs={{0,1},{1,0},{2,3},{3,2},{4,5},{5,4},{6,7},{7,6},{8,9},{9,8},{10,11... | collective-permute-start | bytes 1376264 | tf_op jit(solution)/shard_map/ppermute | solution.py:434
  59.7 32.8 %collective-permute-start.15 = (bf16[224,1024]{1,0:T(8,128)(2,1)S(1)}, bf16[224,1024]{1,0:T(8,128)(2,1)S(1)}, u32[]{:S(2)}, u32[]{:S(2)}) collective-permute-start(bf16[224,1024]{1,0:T(8,128)(2,1)S(1)} %get-tuple-element.41), channel_id=1, source_target_pairs={{0,1},{1,0},{2,3},{3,2},{4,5},{5,4},{6,7},{7,6},{8,9},{9,8},{10,11... | collective-permute-start | bytes 1376264 | tf_op jit(solution)/shard_map/ppermute | solution.py:434
  61.2 4.0 %copy-start.16 = (f32[336,128]{1,0:T(8,128)}, f32[336,128]{1,0:T(8,128)S(1)}, u32[]{:S(2)}) copy-start(f32[336,128]{1,0:T(8,128)S(1)} %collective-permute-done.4.far_a) | copy-start | bytes 516100
  68.7 6.7 %collective-permute-start.7 = (f32[168,128]{1,0:T(8,128)S(1)}, f32[168,128]{1,0:T(8,128)S(1)}, u32[]{:S(2)}, u32[]{:S(2)}) collective-permute-start(f32[168,128]{1,0:T(8,128)S(1)} %get-tuple-element.70), channel_id=1, source_target_pairs={{0,16},{2,18},{4,20},{6,22},{8,24},{10,26},{12,28},{14,30},{16,0},... | collective-permute-start | bytes 258056 | tf_op jit(solution)/shard_map/ppermute | solution.py:372
  70.3 5.2 %collective-permute-start.8 = (f32[168,128]{1,0:T(8,128)S(1)}, f32[168,128]{1,0:T(8,128)S(1)}, u32[]{:S(2)}, u32[]{:S(2)}) collective-permute-start(f32[168,128]{1,0:T(8,128)S(1)} %get-tuple-element.68), channel_id=1, source_target_pairs={{0,4},{2,6},{4,0},{6,2},{8,12},{10,14},{12,8},{14,10},{16,20},{18,... | collective-permute-start | bytes 258056 | tf_op jit(solution)/shard_map/ppermute | solution.py:372
  77.8 6.5 %collective-permute-start.10 = (f32[168,128]{1,0:T(8,128)}, f32[168,128]{1,0:T(8,128)S(1)}, u32[]{:S(2)}, u32[]{:S(2)}) collective-permute-start(f32[168,128]{1,0:T(8,128)} %get-tuple-element.36.near_a), channel_id=1, source_target_pairs={{0,16},{2,18},{4,20},{6,22},{8,24},{10,26},{12,28},{14,30},{16,0},... | collective-permute-start | bytes 258056 | tf_op jit(solution)/shard_map/ppermute | solution.py:372
  80.0 4.7 %collective-permute-start.11 = (f32[168,128]{1,0:T(8,128)}, f32[168,128]{1,0:T(8,128)S(1)}, u32[]{:S(2)}, u32[]{:S(2)}) collective-permute-start(f32[168,128]{1,0:T(8,128)} %get-tuple-element.37.near_b), channel_id=1, source_target_pairs={{0,4},{2,6},{4,0},{6,2},{8,12},{10,14},{12,8},{14,10},{16,20},{18,... | collective-permute-start | bytes 258056 | tf_op jit(solution)/shard_map/ppermute | solution.py:372
  87.4 7.7 %collective-permute-start.13 = (f32[336,128]{1,0:T(8,128)}, f32[336,128]{1,0:T(8,128)S(1)}, u32[]{:S(2)}, u32[]{:S(2)}) collective-permute-start(f32[336,128]{1,0:T(8,128)} %get-tuple-element.39.near_a), channel_id=1, source_target_pairs={{0,8},{2,10},{4,12},{6,14},{8,0},{10,2},{12,4},{14,6},{16,24},{18,... | collective-permute-start | bytes 516104 | tf_op jit(solution)/shard_map/ppermute | solution.py:372
  89.6 8.6 %collective-permute-start.14 = (f32[336,128]{1,0:T(8,128)}, f32[336,128]{1,0:T(8,128)S(1)}, u32[]{:S(2)}, u32[]{:S(2)}) collective-permute-start(f32[336,128]{1,0:T(8,128)} %get-tuple-element.40.near_b), channel_id=1, source_target_pairs={{0,16},{2,18},{4,20},{6,22},{8,24},{10,26},{12,28},{14,30},{16,0},... | collective-permute-start | bytes 516104 | tf_op jit(solution)/shard_map/ppermute | solution.py:372
  91.0 24.2 %copy-start.24 = (s32[5]{0:T(128)S(1)}, s32[5]{0:T(128)}, u32[]{:S(2)}) copy-start(s32[5]{0:T(128)} %param.5) | copy-start | bytes 64
  91.0 11.4 %collective-permute-start.18 = (bf16[224,1024]{1,0:T(8,128)(2,1)S(1)}, bf16[224,1024]{1,0:T(8,128)(2,1)S(1)}, u32[]{:S(2)}, u32[]{:S(2)}) collective-permute-start(bf16[224,1024]{1,0:T(8,128)(2,1)S(1)} %get-tuple-element.44), channel_id=1, source_target_pairs={{0,1},{1,0},{2,3},{3,2},{4,5},{5,4},{6,7},{7,6},{8,9},{9,8},{10,11... | collective-permute-start | bytes 1376264 | tf_op jit(solution)/shard_map/ppermute | solution.py:434
  92.5 5.7 %copy-start.10 = (bf16[224,1024]{1,0:T(8,128)(2,1)}, bf16[224,1024]{1,0:T(8,128)(2,1)S(1)}, u32[]{:S(2)}) copy-start(bf16[224,1024]{1,0:T(8,128)(2,1)S(1)} %collective-permute-done.15.refs_0_.refs_4_) | copy-start | bytes 1376260
  95.1 3.1 %copy-start.17 = (f32[336,128]{1,0:T(8,128)}, f32[336,128]{1,0:T(8,128)S(1)}, u32[]{:S(2)}) copy-start(f32[336,128]{1,0:T(8,128)S(1)} %collective-permute-done.13.far_a) | copy-start | bytes 516100
  100.9 7.5 %collective-permute-start.16 = (f32[672,128]{1,0:T(8,128)}, f32[672,128]{1,0:T(8,128)S(1)}, u32[]{:S(2)}, u32[]{:S(2)}) collective-permute-start(f32[672,128]{1,0:T(8,128)} %get-tuple-element.42.near_a), channel_id=1, source_target_pairs={{0,4},{2,6},{4,0},{6,2},{8,12},{10,14},{12,8},{14,10},{16,20},{18,... | collective-permute-start | bytes 1032200 | tf_op jit(solution)/shard_map/ppermute | solution.py:372
  102.5 7.5 %collective-permute-start.17 = (f32[672,128]{1,0:T(8,128)}, f32[672,128]{1,0:T(8,128)S(1)}, u32[]{:S(2)}, u32[]{:S(2)}) collective-permute-start(f32[672,128]{1,0:T(8,128)} %get-tuple-element.43.near_b), channel_id=1, source_target_pairs={{0,8},{2,10},{4,12},{6,14},{8,0},{10,2},{12,4},{14,6},{16,24},{18,... | collective-permute-start | bytes 1032200 | tf_op jit(solution)/shard_map/ppermute | solution.py:372
  102.5 7.5 %copy-start.11 = (bf16[224,1024]{1,0:T(8,128)(2,1)}, bf16[224,1024]{1,0:T(8,128)(2,1)S(1)}, u32[]{:S(2)}) copy-start(bf16[224,1024]{1,0:T(8,128)(2,1)S(1)} %collective-permute-done.18.refs_0_.refs_5_) | copy-start | bytes 1376260
  108.4 1.5 copy-start.14
  113.2 2.6 %collective-permute-start.19 = (f32[1344,128]{1,0:T(8,128)}, f32[1344,128]{1,0:T(8,128)S(1)}, u32[]{:S(2)}, u32[]{:S(2)}) collective-permute-start(f32[1344,128]{1,0:T(8,128)} %get-tuple-element.45.near_a), channel_id=1, source_target_pairs={{0,2},{2,0},{4,6},{6,4},{8,10},{10,8},{12,14},{14,12},{16,18},{18,... | collective-permute-start | bytes 2064392 | tf_op jit(solution)/shard_map/ppermute | solution.py:372
  113.2 3.3 %collective-permute-start.20 = (f32[1344,128]{1,0:T(8,128)}, f32[1344,128]{1,0:T(8,128)S(1)}, u32[]{:S(2)}, u32[]{:S(2)}) collective-permute-start(f32[1344,128]{1,0:T(8,128)} %get-tuple-element.46.near_b), channel_id=1, source_target_pairs={{0,2},{2,0},{4,6},{6,4},{8,10},{10,8},{12,14},{14,12},{16,18},{18,... | collective-permute-start | bytes 2064392 | tf_op jit(solution)/shard_map/ppermute | solution.py:372
  113.7 63.2 %collective-permute-start.21 = (bf16[704,1024]{1,0:T(8,128)(2,1)}, bf16[704,1024]{1,0:T(8,128)(2,1)}, u32[]{:S(2)}, u32[]{:S(2)}) collective-permute-start(bf16[704,1024]{1,0:T(8,128)(2,1)} %get-tuple-element.48), channel_id=1, source_target_pairs={{0,1},{1,0},{2,3},{3,2},{4,5},{5,4},{6,7},{7,6},{8,9},{9,8},{10,11... | collective-permute-start | bytes 4325384 | tf_op jit(solution)/shard_map/ppermute | solution.py:489
  116.5 1.1 copy-start.2
  117.6 1.1 copy-start.3
  176.8 9.0 %copy-start.1 = (f32[8,1024]{1,0:T(8,128)}, f32[8,1024]{1,0:T(8,128)S(1)}, u32[]{:S(2)}) copy-start(f32[8,1024]{1,0:T(8,128)S(1)} %get-tuple-element.49.mean_ref) | copy-start | bytes 98308
  178.4 5.8 %collective-permute-start.22 = (bf16[64,1024]{1,0:T(8,128)(2,1)}, bf16[64,1024]{1,0:T(8,128)(2,1)S(1)}, u32[]{:S(2)}, u32[]{:S(2)}) collective-permute-start(bf16[64,1024]{1,0:T(8,128)(2,1)} %after_piece.1), channel_id=1, source_target_pairs={{0,1},{1,0},{2,3},{3,2},{4,5},{5,4},{6,7},{7,6},{8,9},{9,8},{10,11... | collective-permute-start | bytes 393224 | tf_op jit(solution)/shard_map/ppermute | solution.py:499
  185.9 4.0 %collective-permute-start.23 = (f32[8,1024]{1,0:T(8,128)S(1)}, f32[8,1024]{1,0:T(8,128)S(1)}, u32[]{:S(2)}, u32[]{:S(2)}) collective-permute-start(f32[8,1024]{1,0:T(8,128)S(1)} %get-tuple-element.49.mean_ref), channel_id=1, source_target_pairs={{0,1},{1,0},{2,3},{3,2},{4,5},{5,4},{6,7},{7,6},{8,9},{9,8},{10,11... | collective-permute-start | bytes 98312 | tf_op jit(solution)/shard_map/ppermute | solution.py:500
  189.9 15.3 %copy-start.23 = (f32[8,1024]{1,0:T(8,128)}, f32[8,1024]{1,0:T(8,128)S(1)}, u32[]{:S(2)}) copy-start(f32[8,1024]{1,0:T(8,128)S(1)} %collective-permute-done.23.far_mean_ref) | copy-start | bytes 98308
  215.9 3.7 %collective-permute-start.24 = (f32[32,128]{1,0:T(8,128)S(1)}, f32[32,128]{1,0:T(8,128)S(1)}, u32[]{:S(2)}, u32[]{:S(2)}) collective-permute-start(f32[32,128]{1,0:T(8,128)S(1)} %constant_dynamic-slice_fusion), channel_id=1, source_target_pairs={{0,1},{1,0},{2,3},{3,2},{4,5},{5,4},{6,7},{7,6},{8,9},{9,8},{10,11... | collective-permute-start | bytes 49160 | tf_op jit(solution)/shard_map/ppermute | solution.py:508
  220.3 1.2 collective-permute-start.25
  221.5 3.7 %collective-permute-start.26 = (f32[32,128]{1,0:T(8,128)S(1)}, f32[32,128]{1,0:T(8,128)S(1)}, u32[]{:S(2)}, u32[]{:S(2)}) collective-permute-start(f32[32,128]{1,0:T(8,128)S(1)} %add.95), channel_id=1, source_target_pairs={{0,4},{2,6},{4,0},{6,2},{8,12},{10,14},{12,8},{14,10},{16,20},{18,... | collective-permute-start | bytes 49160 | tf_op jit(solution)/shard_map/ppermute | solution.py:372
  225.3 3.7 %collective-permute-start.27 = (f32[32,128]{1,0:T(8,128)S(1)}, f32[32,128]{1,0:T(8,128)S(1)}, u32[]{:S(2)}, u32[]{:S(2)}) collective-permute-start(f32[32,128]{1,0:T(8,128)S(1)} %add.96), channel_id=1, source_target_pairs={{0,8},{2,10},{4,12},{6,14},{8,0},{10,2},{12,4},{14,6},{16,24},{18,... | collective-permute-start | bytes 49160 | tf_op jit(solution)/shard_map/ppermute | solution.py:372
  229.0 4.6 %collective-permute-start.28 = (f32[32,128]{1,0:T(8,128)S(1)}, f32[32,128]{1,0:T(8,128)S(1)}, u32[]{:S(2)}, u32[]{:S(2)}) collective-permute-start(f32[32,128]{1,0:T(8,128)S(1)} %add.97), channel_id=1, source_target_pairs={{0,16},{2,18},{4,20},{6,22},{8,24},{10,26},{12,28},{14,30},{16,0},... | collective-permute-start | bytes 49160 | tf_op jit(solution)/shard_map/ppermute | solution.py:372
  (7 other events, 4.6 us)
Sparse Core Ops, SparseCore 0:
  186.0 19.1 all-gather.2
